TPU v7x, 32 devices: a whole 2x2x4 slice. The times are simulated.
32 devices in a mesh: ctx: 32 (over z, y, x, core), head: 1.
Axes of the slice: x: 2, y: 2, z: 4, core: 2. Of those that a mesh axis runs over, the one named last changes fastest.
Arguments:
- queries: bfloat16 [4096, 4096], P('ctx', 'head'), may hold values from -9 to 9
- key_rows: bfloat16 [4096, 4096], P('ctx', 'head'), may hold values from -9 to 9
- value_rows: bfloat16 [4096, 4096], P('ctx', 'head'), may hold values from -6 to 6
- offsets: int32 [3, 32], P(None, 'head'), may hold values from 0 to 3, as said below
- sublayer_norm_gain: float32 [4096], P('head'), may hold values from 0.25 to 1.75
- cotangent: bfloat16 [4096, 4096], P('ctx', 'head'), may hold values from -6 to 6
Outputs:
- normed: bfloat16 [4096, 4096], P('ctx', 'head')
- query_grad: bfloat16 [4096, 4096], P('ctx', 'head')
- key_grad: bfloat16 [4096, 4096], P('ctx', 'head')
- value_grad: bfloat16 [4096, 4096], P('ctx', 'head')
Inputs may be any that keep to these rules, and one draw needn't show every extreme that they name: Row l holds offsets of 0 to 2**l - 1, and each of these values belongs to exactly 32 / 2**l heads.
All inputs are finite; a program needn't handle non-finite values.
Results may differ from a plain program's by a relative error of at most 0.007.
Values may be sent and summed in bfloat16 or wider, within the bound.
A program may use at most 192 MiB of HBM per device.

v0:
```python
from functools import reduce
import math

import jax
import jax.numpy as jnp
from jax import lax
from jax.sharding import PartitionSpec as P

SEG0 = 512


NEG_FILL = -1e30
EPSILON = 1e-05


def as_sent(x):
    return jax.tree.map(lambda a: a.astype(jnp.bfloat16) if a.dtype == jnp.float32 else a, x)


def from_partner(block, axis, stride):
    count = lax.axis_size(axis)
    route = []
    for low in range(count):
        high = low | 1 << stride
        if high != low and high < count:
            route += [(low, high), (high, low)]
    return lax.ppermute(block, axis, route)


def pick_rows(source, mask_table, stride):
    count = source.shape[0] // stride
    shaped = source.reshape((count, stride) + source.shape[1:])
    chosen = mask_table.reshape((1, stride, mask_table.shape[1]) + (1,) * (source.ndim - 2))
    return jnp.sum(jnp.where(chosen, shaped, jnp.zeros((), source.dtype)), axis=1)


def put_rows(picked, mask_table, stride, filler):
    chosen = mask_table.reshape((1, stride, mask_table.shape[1]) + (1,) * (picked.ndim - 2))
    spread = jnp.where(chosen, picked[:, None], jnp.asarray(filler, picked.dtype))
    return spread.reshape((picked.shape[0] * stride,) + picked.shape[1:])


def swap_keys(members, bit_num):
    return jax.tree.map(
        lambda part, own: part.astype(own.dtype),
        from_partner(as_sent(members), "ctx", bit_num),
        members,
    )


def swap_queries(members, bit_num):
    return jax.tree.map(
        lambda part, own: part.astype(own.dtype),
        from_partner(as_sent(members), "ctx", bit_num),
        members,
    )


def swap_stats(members, bit_num):
    return from_partner(members, "ctx", bit_num)


def doubling(members, group_bits, mover, ctx_index):
    for bit_num in range(group_bits):
        arrived = mover(members, bit_num)
        is_lower = ctx_index >> bit_num & 1 == 0
        members = tuple(
            (
                jnp.where(
                    is_lower,
                    jnp.concatenate([own_part, peer_part], 0),
                    jnp.concatenate([peer_part, own_part], 0),
                )
                for own_part, peer_part in zip(members, arrived)
            )
        )
    return members


def grad_block(
    query_seg, key_seg, value_seg, dout_seg, lse_seg, delta_seg, score_scale, want_query, want_keys
):
    lse_t = jnp.transpose(lse_seg, (0, 2, 1))[..., None]
    delta_t = jnp.transpose(delta_seg, (0, 2, 1))[..., None]
    scores = (
        jnp.einsum("sqhd,skhd->shqk", query_seg, key_seg, preferred_element_type=jnp.float32)
        * score_scale
    )
    probs = jnp.exp(scores - lse_t)
    dprobs = jnp.einsum("sqhd,skhd->shqk", dout_seg, value_seg, preferred_element_type=jnp.float32)
    dscores = (probs * (dprobs - delta_t)).astype(jnp.bfloat16)
    query_part = None
    key_part = None
    value_part = None
    if want_query:
        query_part = (
            jnp.einsum("shqk,skhd->sqhd", dscores, key_seg, preferred_element_type=jnp.float32)
            * score_scale
        )
    if want_keys:
        probs_half = probs.astype(jnp.bfloat16)
        key_part = (
            jnp.einsum("shqk,sqhd->skhd", dscores, query_seg, preferred_element_type=jnp.float32)
            * score_scale
        )
        value_part = jnp.einsum(
            "shqk,sqhd->skhd", probs_half, dout_seg, preferred_element_type=jnp.float32
        )
    return (query_part, key_part, value_part)


def on_device(queries, key_rows, value_rows, offsets, sublayer_norm_gain, cotangent):
    tok_rows = queries.shape[0]
    head_local = offsets.shape[1]
    head_size = queries.shape[1] // head_local
    level_count = offsets.shape[0]
    feature_total_count = lax.axis_size("head") * queries.shape[1]
    ctx_index = lax.axis_index("ctx")
    score_scale = 1.0 / math.sqrt(head_size)
    shape3 = (tok_rows, head_local, head_size)
    query_all = queries.reshape(shape3)
    key_all = key_rows.reshape(shape3)
    value_all = value_rows.reshape(shape3)

    def level_layout(level_num):
        stride = 2**level_num
        picked_rows = tok_rows // stride
        group_size = max(1, SEG0 * stride // tok_rows)
        group_bits = group_size.bit_length() - 1
        seg_count = max(1, picked_rows // SEG0)
        mask_table = jnp.arange(stride, dtype=jnp.int32)[:, None] == offsets[level_num][None, :]
        return (stride, picked_rows, group_bits, seg_count, mask_table)

    stored = []
    maxima = []
    totals = []
    partials = []
    for level_num in range(level_count):
        stride, picked_rows, group_bits, seg_count, mask_table = level_layout(level_num)
        query_sel = pick_rows(query_all, mask_table, stride)
        key_sel = pick_rows(key_all, mask_table, stride)
        value_sel = pick_rows(value_all, mask_table, stride)
        key_group, value_group = doubling((key_sel, value_sel), group_bits, swap_keys, ctx_index)
        stored.append((key_group, value_group))
        query_seg = query_sel.reshape(seg_count, -1, head_local, head_size)
        key_seg = key_group.reshape(seg_count, SEG0, head_local, head_size)
        value_seg = value_group.reshape(seg_count, SEG0, head_local, head_size)
        scores = (
            jnp.einsum("sqhd,skhd->shqk", query_seg, key_seg, preferred_element_type=jnp.float32)
            * score_scale
        )
        row_max = jnp.max(scores, axis=-1)
        weights = jnp.exp(scores - row_max[..., None])
        row_total = jnp.sum(weights, axis=-1)
        level_out = jnp.einsum(
            "shqk,skhd->sqhd",
            weights.astype(jnp.bfloat16),
            value_seg,
            preferred_element_type=jnp.float32,
        )
        flat_max = jnp.transpose(row_max, (0, 2, 1)).reshape(picked_rows, head_local)
        flat_total = jnp.transpose(row_total, (0, 2, 1)).reshape(picked_rows, head_local)
        maxima.append(put_rows(flat_max, mask_table, stride, NEG_FILL))
        totals.append(put_rows(flat_total, mask_table, stride, 0.0))
        partials.append(
            put_rows(level_out.reshape(picked_rows, head_local, head_size), mask_table, stride, 0.0)
        )
    top_max = reduce(jnp.maximum, maxima)
    factors = [jnp.exp(each_max - top_max) for each_max in maxima]
    total = factors[0] * totals[0]
    summed = factors[0][..., None] * partials[0]
    for level_num in range(1, level_count):
        total = total + factors[level_num] * totals[level_num]
        summed = summed + factors[level_num][..., None] * partials[level_num]
    attended = (summed / total[..., None]).astype(jnp.bfloat16)
    log_total = top_max + jnp.log(total)
    attended_rows_flattened = attended.reshape(tok_rows, -1).astype(jnp.float32)
    first_sum, second_sum = lax.psum(
        (
            jnp.sum(attended_rows_flattened, axis=1),
            jnp.sum(attended_rows_flattened * attended_rows_flattened, axis=1),
        ),
        "head",
    )
    feature_mean = first_sum / feature_total_count
    variance = second_sum / feature_total_count - feature_mean * feature_mean
    inverse_deviation = 1.0 / jnp.sqrt(variance + EPSILON)
    normalized_input = (attended_rows_flattened - feature_mean[:, None]) * inverse_deviation[
        :, None
    ]
    normed = (normalized_input * sublayer_norm_gain[None, :]).astype(jnp.bfloat16)
    normalized_gradient = cotangent.astype(jnp.float32) * sublayer_norm_gain[None, :]
    gradient_sum_first, gradient_sum_second = lax.psum(
        (
            jnp.sum(normalized_gradient, axis=1),
            jnp.sum(normalized_gradient * normalized_input, axis=1),
        ),
        "head",
    )
    attended_gradient = (
        (
            normalized_gradient
            - gradient_sum_first[:, None] / feature_total_count
            - normalized_input * gradient_sum_second[:, None] / feature_total_count
        )
        * inverse_deviation[:, None]
    ).astype(jnp.bfloat16)
    dout_all = attended_gradient.reshape(shape3)
    delta = jnp.sum(dout_all.astype(jnp.float32) * attended.astype(jnp.float32), axis=-1)
    query_acc = jnp.zeros(shape3, jnp.float32)
    key_acc = jnp.zeros(shape3, jnp.float32)
    value_acc = jnp.zeros(shape3, jnp.float32)
    for level_num in range(level_count):
        stride, picked_rows, group_bits, seg_count, mask_table = level_layout(level_num)
        query_sel = pick_rows(query_all, mask_table, stride)
        key_sel = pick_rows(key_all, mask_table, stride)
        value_sel = pick_rows(value_all, mask_table, stride)
        dout_sel = pick_rows(dout_all, mask_table, stride)
        lse_sel = pick_rows(log_total, mask_table, stride)
        delta_sel = pick_rows(delta, mask_table, stride)
        key_group, value_group = stored[level_num]
        query_seg = query_sel.reshape(seg_count, -1, head_local, head_size)
        dout_seg = dout_sel.reshape(seg_count, -1, head_local, head_size)
        lse_seg = lse_sel.reshape(seg_count, -1, head_local)
        delta_seg = delta_sel.reshape(seg_count, -1, head_local)
        key_seg = key_group.reshape(seg_count, SEG0, head_local, head_size)
        value_seg = value_group.reshape(seg_count, SEG0, head_local, head_size)
        query_part, unused_key, unused_value = grad_block(
            query_seg, key_seg, value_seg, dout_seg, lse_seg, delta_seg, score_scale, True, False
        )
        query_group, dout_group = doubling(
            (query_sel, dout_sel), group_bits, swap_queries, ctx_index
        )
        lse_group, delta_group = doubling((lse_sel, delta_sel), group_bits, swap_stats, ctx_index)
        unused_query, key_part, value_part = grad_block(
            query_group.reshape(seg_count, SEG0, head_local, head_size),
            key_sel.reshape(seg_count, -1, head_local, head_size),
            value_sel.reshape(seg_count, -1, head_local, head_size),
            dout_group.reshape(seg_count, SEG0, head_local, head_size),
            lse_group.reshape(seg_count, SEG0, head_local),
            delta_group.reshape(seg_count, SEG0, head_local),
            score_scale,
            False,
            True,
        )
        key_own = key_part.reshape(picked_rows, head_local, head_size)
        value_own = value_part.reshape(picked_rows, head_local, head_size)
        query_acc = query_acc + put_rows(
            query_part.reshape(picked_rows, head_local, head_size), mask_table, stride, 0.0
        )
        key_acc = key_acc + put_rows(key_own, mask_table, stride, 0.0)
        value_acc = value_acc + put_rows(value_own, mask_table, stride, 0.0)
    flat_shape = (tok_rows, head_local * head_size)
    query_grad = query_acc.astype(jnp.bfloat16).reshape(flat_shape)
    key_grad = key_acc.astype(jnp.bfloat16).reshape(flat_shape)
    value_grad = value_acc.astype(jnp.bfloat16).reshape(flat_shape)
    return (normed, query_grad, key_grad, value_grad)


def solution(mesh):
    in_specs = (
        P("ctx", "head"),
        P("ctx", "head"),
        P("ctx", "head"),
        P(None, "head"),
        P("head"),
        P("ctx", "head"),
    )
    out_specs = (P("ctx", "head"), P("ctx", "head"), P("ctx", "head"), P("ctx", "head"))
    return jax.shard_map(
        on_device, mesh=mesh, in_specs=in_specs, out_specs=out_specs, check_vma=False
    )
```

profile of v0, /device:TPU:1, one launch (start us, length us, event | category | flops | bytes accessed | tf_op | source)
XLA Modules:
  0.0 706.1 jit_solution(10848534825432302998)
XLA Ops:
  15.9 3.1 broadcast_select_fusion.1
  21.8 2.7 collective-permute-start.15
  27.9 2.3 copy.328
  31.2 2.3 copy.323
  39.7 8.6 %collective-permute-done.6 = bf16[64,32,128]{2,1,0:T(8,128)(2,1)} collective-permute-done((bf16[64,32,128]{2,1,0:T(8,128)(2,1)}, bf16[64,32,128]{2,1,0:T(8,128)(2,1)}, u32[]{:S(2)}, u32[]{:S(2)}) %collective-permute-start.6) | collective-permute-done | bytes 524320 | tf_op jit(solution)/shard_map/ppermute | solution.py:27
  52.9 2.5 maximum_select_fusion.12
  55.4 4.0 collective-permute-done.39
  66.0 3.9 maximum_select_fusion.15
  69.9 12.0 %collective-permute-done.3 = bf16[128,32,128]{2,1,0:T(8,128)(2,1)S(1)} collective-permute-done((bf16[128,32,128]{2,1,0:T(8,128)(2,1)S(1)}, bf16[128,32,128]{2,1,0:T(8,128)(2,1)S(1)}, u32[]{:S(2)}, u32[]{:S(2)}) %collective-permute-start.3) | collective-permute-done | bytes 1048608 | tf_op jit(solution)/shard_map/ppermute | solution.py:27
  83.2 2.3 maximum_select_fusion.18
  85.5 18.9 %collective-permute-done.12 = bf16[128,32,128]{2,1,0:T(8,128)(2,1)S(1)} collective-permute-done((bf16[128,32,128]{2,1,0:T(8,128)(2,1)S(1)}, bf16[128,32,128]{2,1,0:T(8,128)(2,1)S(1)}, u32[]{:S(2)}, u32[]{:S(2)}) %collective-permute-start.12) | collective-permute-done | bytes 1048608 | tf_op jit(solution)/shard_map/ppermute | solution.py:27
  107.3 19.5 %collective-permute-done.27 = bf16[128,32,128]{2,1,0:T(8,128)(2,1)S(1)} collective-permute-done((bf16[128,32,128]{2,1,0:T(8,128)(2,1)S(1)}, bf16[128,32,128]{2,1,0:T(8,128)(2,1)S(1)}, u32[]{:S(2)}, u32[]{:S(2)}) %collective-permute-start.27) | collective-permute-done | bytes 1048608 | tf_op jit(solution)/shard_map/ppermute | solution.py:27
  136.7 35.1 %collective-permute-done.1 = bf16[256,32,128]{0,2,1:T(8,128)(2,1)S(1)} collective-permute-done((bf16[256,32,128]{0,2,1:T(8,128)(2,1)S(1)}, bf16[256,32,128]{0,2,1:T(8,128)(2,1)S(1)}, u32[]{:S(2)}, u32[]{:S(2)}) %collective-permute-start.1) | collective-permute-done | bytes 2097184 | tf_op jit(solution)/shard_map/ppermute | solution.py:27
  174.5 4.5 multiply_reduce_fusion
  183.9 32.9 %collective-permute-done.19 = bf16[256,32,128]{0,2,1:T(8,128)(2,1)} collective-permute-done((bf16[256,32,128]{0,2,1:T(8,128)(2,1)}, bf16[256,32,128]{0,2,1:T(8,128)(2,1)}, u32[]{:S(2)}, u32[]{:S(2)}) %collective-permute-start.19) | collective-permute-done | bytes 2097184 | tf_op jit(solution)/shard_map/ppermute | solution.py:27
  218.2 8.6 %fusion.164 = f32[32,512,128]{2,1,0:T(8,128)} fusion(bf16[128,32,128]{0,2,1:T(8,128)(2,1)} %copy-done.18, bf16[256,32,128]{0,2,1:T(8,128)(2,1)} %collective-permute-done.19, bf16[256,32,128]{0,2,1:T(8,128)(2,1)} %maximum_select_fusion.18, pred[]{:T(512)S(6)} %eq.39), kind=kOutput, calls=%fused_computation.184 | convolution fusion | flops 555745280 | bytes 13631489 | tf_op jit(solution)/shard_map/sqhd,skhd->shqk/dot_general | solution.py:86
  226.9 4.0 maximum_select_fusion.1
  231.0 4.9 multiply_reduce_fusion.1
  237.3 2.6 maximum_select_fusion.4
  239.9 5.3 fusion.110
  246.2 2.4 copy.337
  248.6 3.2 fusion.23
  254.0 13.9 %collective-permute-done.28 = bf16[256,32,128]{2,1,0:T(8,128)(2,1)} collective-permute-done((bf16[256,32,128]{2,1,0:T(8,128)(2,1)}, bf16[256,32,128]{2,1,0:T(8,128)(2,1)}, u32[]{:S(2)}, u32[]{:S(2)}) %collective-permute-start.28) | collective-permute-done | bytes 2097184 | tf_op jit(solution)/shard_map/ppermute | solution.py:27
  267.9 3.9 maximum_select_fusion.8
  271.8 6.7 fusion.33
  278.5 30.0 %collective-permute-done.8 = bf16[256,32,128]{2,1,0:T(8,128)(2,1)} collective-permute-done((bf16[256,32,128]{2,1,0:T(8,128)(2,1)}, bf16[256,32,128]{2,1,0:T(8,128)(2,1)}, u32[]{:S(2)}, u32[]{:S(2)}) %collective-permute-start.8) | collective-permute-done | bytes 2097184 | tf_op jit(solution)/shard_map/ppermute | solution.py:27
  308.5 4.0 maximum_select_fusion.2
  312.4 5.8 multiply_reduce_fusion.3
  318.3 4.4 maximum_select_fusion.5
  322.7 4.7 fusion.140
  329.4 3.0 copy.338
  334.0 11.1 %convert_reduce_fusion = (f32[128]{0:T(128)}, f32[128]{0:T(128)}, bf16[128,32,128]{0,2,1:T(8,128)(2,1)}, f32[32,128,128]{2,1,0:T(8,128)}) fusion(f32[128,32]{0,1:T(8,128)S(1)} %get-tuple-element.19, f32[128,32,128]{0,2,1:T(8,128)} %copy.338, pred[128,32]{0,1:T(8,128)(4,1)S(1)} %copy-done.58, f32[128,32]{0,1:T(8,128)S(1)} %get-tuple-element.21, ...), kind=kOutput, calls=%fused_computation.78 | convolution fusion | flops 569376512 | bytes 20014112 | tf_op jit(solution)/shard_map/shqk,skhd->sqhd/dot_general | solution.py:155
  345.2 2.9 copy.318
  349.6 2.9 copy.319
  353.9 2.9 copy.324
  358.3 2.9 copy.329
  361.2 2.4 div.33
  363.6 2.9 copy.336
  367.2 9.3 %fusion.87 = (f32[128]{0:T(128)S(1)}, f32[128]{0:T(128)S(1)}, bf16[128,4096]{1,0:T(8,128)(2,1)S(1)}) fusion(bf16[128,4096]{1,0:T(8,128)(2,1)} %param.11, f32[4096]{0:T(1024)} %param.10, f32[128]{0:T(128)S(1)} %get-tuple-element.39, f32[128]{0:T(128)S(1)} %get-tuple-element.38, f32[128,4096]{1,0:T(8,128)} %copy.336, f32[128,4096]{1,0:T(8,128)} %copy.329, ...), kind=kLoop, calls=%fused_computation.133 | loop fusion | flops 9436928 | bytes 17848320 | tf_op jit(solution)/shard_map/reduce_sum | solution.py:195
  376.5 2.4 multiply_convert_fusion.10
  400.3 2.3 select_reduce_fusion.9
  407.3 3.0 collective-permute-start.42
  416.3 13.6 %fusion.149 = f32[32,32,128]{2,0,1:T(8,128)} fusion(bf16[512,32,128]{2,1,0:T(8,128)(2,1)} %copy-done.5, f32[32,32,512]{2,1,0:T(8,128)S(1)} %get-tuple-element.48, bf16[512,32,128]{2,1,0:T(8,128)(2,1)} %copy-done.7, f32[32,32]{1,0:T(8,128)S(1)} %copy.380, f32[32,32]{1,0:T(8,128)S(1)} %copy.376, bf16[32,32,128]{2,1,0:T(8,128)(2,1)} %select_reduce_fusion), kind=kOutput, calls=%fused_computation.157 | convolution fusion | flops 271187968 | bytes 11280384 | tf_op jit(solution)/shard_map/shqk,skhd->sqhd/dot_general | solution.py:97
  429.9 15.5 %fusion.125 = f32[64,32,128]{2,0,1:T(8,128)} fusion(bf16[512,32,128]{2,1,0:T(8,128)(2,1)} %copy-done.3, f32[32,64,512]{2,1,0:T(8,128)} %copy-done, f32[32,64]{1,0:T(8,128)S(1)} %bitcast.400, f32[32,64]{1,0:T(8,128)S(1)} %bitcast.399, bf16[512,32,128]{2,1,0:T(8,128)(2,1)} %copy-done.4, bf16[64,32,128]{2,1,0:T(8,128)(2,1)} %select_reduce_fusion.1), kind=kOutput, calls=%fused_computation.151 | convolution fusion | flops 542375936 | bytes 14172160 | tf_op jit(solution)/shard_map/shqk,skhd->sqhd/dot_general | solution.py:97
  445.9 5.2 maximum_select_fusion.10
  451.1 11.2 %fusion.109 = f32[32,128,128]{2,1,0:T(8,128)} fusion(f32[32,128,512]{2,1,0:T(8,128)} %copy-done.11, f32[32,128]{1,0:T(8,128)S(1)} %get-tuple-element.37, f32[32,128]{1,0:T(8,128)S(1)} %get-tuple-element.36, bf16[128,32,128]{0,2,1:T(8,128)(2,1)S(1)} %copy-done.20, bf16[256,32,128]{0,2,1:T(8,128)(2,1)} %collective-permute-done.10, ...), kind=kOutput, calls=%fused_computation.147 | convolution fusion | flops 1122500608 | bytes 19955712 | tf_op jit(solution)/shard_map/shqk,skhd->sqhd/dot_general | solution.py:97
  462.4 7.9 %fusion.25 = f32[32,512,32]{1,2,0:T(8,128)} fusion(bf16[512,32,128]{2,1,0:T(8,128)(2,1)} %maximum_select_fusion.10, bf16[32,32,128]{2,1,0:T(8,128)(2,1)S(1)} %get-tuple-element.16), kind=kOutput, calls=%fused_computation.42 | convolution fusion | flops 134217728 | bytes 6553600 | tf_op jit(solution)/shard_map/sqhd,skhd->shqk/dot_general | solution.py:86
  471.7 2.3 copy.350
  474.0 2.9 copy.370
  491.6 2.4 maximum_select_fusion.19
  501.9 50.2 %collective-permute-done.30 = f32[128,32]{0,1:T(8,128)S(1)} collective-permute-done((f32[128,32]{0,1:T(8,128)S(1)}, f32[128,32]{0,1:T(8,128)S(1)}, u32[]{:S(2)}, u32[]{:S(2)}) %collective-permute-start.30) | collective-permute-done | bytes 16416 | tf_op jit(solution)/shard_map/ppermute | solution.py:27
  555.5 20.3 %collective-permute-done.25 = f32[256,32]{0,1:T(8,128)S(1)} collective-permute-done((f32[256,32]{0,1:T(8,128)S(1)}, f32[256,32]{0,1:T(8,128)S(1)}, u32[]{:S(2)}, u32[]{:S(2)}) %collective-permute-start.25) | collective-permute-done | bytes 32800 | tf_op jit(solution)/shard_map/ppermute | solution.py:27
  588.6 13.2 %fusion.108 = f32[32,128,128]{2,1,0:T(8,128)} fusion(f32[32,512,128]{2,1,0:T(8,128)} %fusion.164, f32[32,512]{1,0:T(8,128)S(1)} %fusion.183, f32[32,512]{1,0:T(8,128)S(1)} %fusion.182, bf16[128,32,128]{0,2,1:T(8,128)(2,1)S(1)} %copy-done.17, bf16[256,32,128]{0,2,1:T(8,128)(2,1)} %collective-permute-done.23, bf16[256,32,128]{0,2,1:T(8,128)(2,1)} %copy-done.31, ...), kind=kOutput, calls=%fused_computation.146 | convolution fusion | flops 1122500608 | bytes 20054016 | tf_op jit(solution)/shard_map/shqk,sqhd->skhd/dot_general | solution.py:103
  601.8 8.7 %fusion.3 = f32[32,128,128]{2,1,0:T(8,128)} fusion(f32[32,512,128]{2,1,0:T(8,128)} %fusion.164, f32[32,512]{1,0:T(8,128)S(1)} %fusion.182, bf16[256,32,128]{0,2,1:T(8,128)(2,1)} %collective-permute-done.23, bf16[256,32,128]{0,2,1:T(8,128)(2,1)} %copy-done.31, pred[]{:T(512)S(6)} %eq.39), kind=kOutput, calls=%fused_computation.8 | convolution fusion | flops 562036736 | bytes 14745601 | tf_op jit(solution)/shard_map/shqk,sqhd->skhd/dot_general | solution.py:106
  610.5 2.9 copy.388
  613.4 2.9 copy.419
  616.3 12.0 %collective-permute-done.34 = bf16[256,32,128]{2,1,0:T(8,128)(2,1)} collective-permute-done((bf16[256,32,128]{2,1,0:T(8,128)(2,1)}, bf16[256,32,128]{2,1,0:T(8,128)(2,1)}, u32[]{:S(2)}, u32[]{:S(2)}) %collective-permute-start.34) | collective-permute-done | bytes 2097184 | tf_op jit(solution)/shard_map/ppermute | solution.py:27
  628.3 5.4 maximum_select_fusion.9
  633.7 14.4 %fusion.135 = f32[64,32,128]{2,0,1:T(8,128)S(1)} fusion(bf16[512,32,128]{2,1,0:T(8,128)(2,1)} %copy-done.2, f32[32,512,64]{1,2,0:T(8,128)} %fusion.33, f32[32,512]{1,0:T(8,128)S(1)} %fusion.185, f32[32,512]{1,0:T(8,128)S(1)} %fusion.184, bf16[512,32,128]{2,1,0:T(8,128)(2,1)} %maximum_select_fusion.9, bf16[64,32,128]{2,1,0:T(8,128)(2,1)} %get-tuple-element.12), kind=kOutput, calls=%fused_computation.153 | convolution fusion | flops 542375936 | bytes 14286848 | tf_op jit(solution)/shard_map/shqk,sqhd->skhd/dot_general | solution.py:103
  649.7 8.3 %fusion.115 = f32[64,32,128]{2,0,1:T(8,128)S(1)} fusion(bf16[512,32,128]{2,1,0:T(8,128)(2,1)} %maximum_select_fusion.9, f32[32,512,64]{1,2,0:T(8,128)} %fusion.33, f32[32,512]{1,0:T(8,128)S(1)} %fusion.184), kind=kOutput, calls=%fused_computation.149 | convolution fusion | flops 271581184 | bytes 9502720 | tf_op jit(solution)/shard_map/shqk,sqhd->skhd/dot_general | solution.py:106
  659.5 4.1 maximum_select_fusion.11
  665.6 5.2 fusion.143
  670.8 14.3 %fusion.155 = f32[32,32,128]{2,0,1:T(8,128)} fusion(bf16[512,32,128]{2,1,0:T(8,128)(2,1)} %maximum_select_fusion.10, f32[32,512,32]{1,2,0:T(8,128)} %fusion.25, bf16[512,32,128]{2,1,0:T(8,128)(2,1)} %copy-done.6, f32[32,512]{1,0:T(8,128)S(1)} %fusion.187, f32[32,512]{1,0:T(8,128)S(1)} %fusion.186, bf16[32,32,128]{2,1,0:T(8,128)(2,1)} %get-tuple-element.15), kind=kOutput, calls=%fused_computation.159 | convolution fusion | flops 271187968 | bytes 11403264 | tf_op jit(solution)/shard_map/shqk,sqhd->skhd/dot_general | solution.py:103
  691.3 14.6 %fusion.63 = (bf16[128,4096]{1,0:T(8,128)(2,1)}, bf16[128,4096]{1,0:T(8,128)(2,1)}, bf16[128,4096]{1,0:T(8,128)(2,1)}) fusion(pred[128,4096]{1,0:T(8,128)(4,1)S(1)} %copy-done.13, f32[16,8,32,128]{3,2,1,0:T(8,128)S(1)} %bitcast.356, pred[128,4096]{1,0:T(8,128)(4,1)S(1)} %copy-done.15, f32[16,8,32,128]{3,2,1,0:T(8,128)S(1)} %bitcast.359, ...), kind=kLoop, calls=%fused_computation.83 | loop fusion | flops 9437184 | bytes 23072768 | tf_op jit(solution)/shard_map/convert_element_type | solution.py:256
  (360 shorter events, 159.7 us)
Async XLA Ops:
  1.4 25.3 %copy-start.64 = (pred[2,32]{1,0:T(4,128)(4,1)}, pred[2,32]{1,0:T(4,128)(4,1)S(1)}, u32[]{:S(2)}) copy-start(pred[2,32]{1,0:T(4,128)(4,1)S(1)} %iota_compare_fusion.1) | copy-start | bytes 196
  6.8 17.7 %collective-permute-start.2 = (bf16[64,32,128]{2,1,0:T(8,128)(2,1)S(1)}, bf16[64,32,128]{2,1,0:T(8,128)(2,1)}, u32[]{:S(2)}, u32[]{:S(2)}) collective-permute-start(bf16[64,32,128]{2,1,0:T(8,128)(2,1)S(1)} %get-tuple-element.13), channel_id=1, source_target_pairs={{0,1},{1,0},{2,3},{3,2},{4,5},{5,4},{6,7},{7,6},{8,9},{9,8},{10,11... | collective-permute-start | bytes 1572872 | tf_op jit(solution)/shard_map/ppermute | solution.py:27
  6.8 19.8 %collective-permute-start.11 = (bf16[64,32,128]{2,1,0:T(8,128)(2,1)}, bf16[64,32,128]{2,1,0:T(8,128)(2,1)}, u32[]{:S(2)}, u32[]{:S(2)}) collective-permute-start(bf16[64,32,128]{2,1,0:T(8,128)(2,1)} %get-tuple-element.12), channel_id=1, source_target_pairs={{0,1},{1,0},{2,3},{3,2},{4,5},{5,4},{6,7},{7,6},{8,9},{9,8},{10,11... | collective-permute-start | bytes 1572872 | tf_op jit(solution)/shard_map/ppermute | solution.py:27
  9.3 9.7 %collective-permute-start.14 = (bf16[32,32,128]{2,1,0:T(8,128)(2,1)}, bf16[32,32,128]{2,1,0:T(8,128)(2,1)}, u32[]{:S(2)}, u32[]{:S(2)}) collective-permute-start(bf16[32,32,128]{2,1,0:T(8,128)(2,1)} %get-tuple-element.15), channel_id=1, source_target_pairs={{0,1},{1,0},{2,3},{3,2},{4,5},{5,4},{6,7},{7,6},{8,9},{9,8},{10,11... | collective-permute-start | bytes 786440 | tf_op jit(solution)/shard_map/ppermute | solution.py:27
  9.4 10.2 %collective-permute-start.5 = (bf16[32,32,128]{2,1,0:T(8,128)(2,1)S(1)}, bf16[32,32,128]{2,1,0:T(8,128)(2,1)}, u32[]{:S(2)}, u32[]{:S(2)}) collective-permute-start(bf16[32,32,128]{2,1,0:T(8,128)(2,1)S(1)} %get-tuple-element.16), channel_id=1, source_target_pairs={{0,1},{1,0},{2,3},{3,2},{4,5},{5,4},{6,7},{7,6},{8,9},{9,8},{10,11... | collective-permute-start | bytes 786440 | tf_op jit(solution)/shard_map/ppermute | solution.py:27
  9.8 12.0 %collective-permute-start.38 = (bf16[32,32,128]{2,1,0:T(8,128)(2,1)}, bf16[32,32,128]{2,1,0:T(8,128)(2,1)}, u32[]{:S(2)}, u32[]{:S(2)}) collective-permute-start(bf16[32,32,128]{2,1,0:T(8,128)(2,1)} %get-tuple-element.17), channel_id=1, source_target_pairs={{0,1},{1,0},{2,3},{3,2},{4,5},{5,4},{6,7},{7,6},{8,9},{9,8},{10,11... | collective-permute-start | bytes 786440 | tf_op jit(solution)/shard_map/ppermute | solution.py:27
  10.6 23.7 %copy-start.61 = (pred[32]{0:T(512)(128)(4,1)}, pred[32]{0:T(512)(128)(4,1)S(1)}, u32[]{:S(2)}) copy-start(pred[32]{0:T(512)(128)(4,1)S(1)} %compare_bitcast_fusion) | copy-start | bytes 100
  19.0 33.9 %copy-start.18 = (bf16[128,32,128]{0,2,1:T(8,128)(2,1)}, bf16[128,32,128]{0,2,1:T(8,128)(2,1)S(1)}, u32[]{:S(2)}) copy-start(bf16[128,32,128]{0,2,1:T(8,128)(2,1)S(1)} %get-tuple-element.41) | copy-start | bytes 3145732
  19.0 47.0 %copy-start.16 = (bf16[128,32,128]{0,2,1:T(8,128)(2,1)}, bf16[128,32,128]{0,2,1:T(8,128)(2,1)S(1)}, u32[]{:S(2)}) copy-start(bf16[128,32,128]{0,2,1:T(8,128)(2,1)S(1)} %get-tuple-element.40) | copy-start | bytes 3145732
  19.0 15.9 %collective-permute-start.26 = (bf16[64,32,128]{2,1,0:T(8,128)(2,1)S(1)}, bf16[64,32,128]{2,1,0:T(8,128)(2,1)}, u32[]{:S(2)}, u32[]{:S(2)}) collective-permute-start(bf16[64,32,128]{2,1,0:T(8,128)(2,1)S(1)} %get-tuple-element.14), channel_id=1, source_target_pairs={{0,1},{1,0},{2,3},{3,2},{4,5},{5,4},{6,7},{7,6},{8,9},{9,8},{10,11... | collective-permute-start | bytes 1572872 | tf_op jit(solution)/shard_map/ppermute | solution.py:27
  19.5 33.1 %collective-permute-start = (bf16[128,32,128]{0,2,1:T(8,128)(2,1)S(1)}, bf16[128,32,128]{0,2,1:T(8,128)(2,1)}, u32[]{:S(2)}, u32[]{:S(2)}) collective-permute-start(bf16[128,32,128]{0,2,1:T(8,128)(2,1)S(1)} %get-tuple-element.41), channel_id=1, source_target_pairs={{0,1},{1,0},{2,3},{3,2},{4,5},{5,4},{6,7},{7,6},{8,9},{9,8},{10,11... | collective-permute-start | bytes 3145736 | tf_op jit(solution)/shard_map/ppermute | solution.py:27
  21.8 15.3 %collective-permute-start.15 = (bf16[64,32,128]{2,1,0:T(8,128)(2,1)}, bf16[64,32,128]{2,1,0:T(8,128)(2,1)}, u32[]{:S(2)}, u32[]{:S(2)}) collective-permute-start(bf16[64,32,128]{2,1,0:T(8,128)(2,1)} %maximum_select_fusion.43), channel_id=1, source_target_pairs={{0,2},{2,0},{1,3},{3,1},{4,6},{6,4},{5,7},{7,5},{8,10},{10,8},{9,1... | collective-permute-start | bytes 1572872 | tf_op jit(solution)/shard_map/ppermute | solution.py:27
  24.4 36.2 %collective-permute-start.9 = (bf16[128,32,128]{0,2,1:T(8,128)(2,1)S(1)}, bf16[128,32,128]{0,2,1:T(8,128)(2,1)}, u32[]{:S(2)}, u32[]{:S(2)}) collective-permute-start(bf16[128,32,128]{0,2,1:T(8,128)(2,1)S(1)} %get-tuple-element.40), channel_id=1, source_target_pairs={{0,1},{1,0},{2,3},{3,2},{4,5},{5,4},{6,7},{7,6},{8,9},{9,8},{10,11... | collective-permute-start | bytes 3145736 | tf_op jit(solution)/shard_map/ppermute | solution.py:27
  26.6 21.6 %collective-permute-start.6 = (bf16[64,32,128]{2,1,0:T(8,128)(2,1)}, bf16[64,32,128]{2,1,0:T(8,128)(2,1)}, u32[]{:S(2)}, u32[]{:S(2)}) collective-permute-start(bf16[64,32,128]{2,1,0:T(8,128)(2,1)} %maximum_select_fusion.42), channel_id=1, source_target_pairs={{0,2},{2,0},{1,3},{3,1},{4,6},{6,4},{5,7},{7,5},{8,10},{10,8},{9,1... | collective-permute-start | bytes 1572872 | tf_op jit(solution)/shard_map/ppermute | solution.py:27
  26.8 24.4 %copy-start.57 = (pred[128,32]{0,1:T(8,128)(4,1)}, pred[128,32]{0,1:T(8,128)(4,1)S(1)}, u32[]{:S(2)}) copy-start(pred[128,32]{0,1:T(8,128)(4,1)S(1)} %copy.315) | copy-start | bytes 12292
  27.0 24.3 %copy-start.59 = (pred[128,32]{0,1:T(8,128)(4,1)}, pred[128,32]{0,1:T(8,128)(4,1)S(1)}, u32[]{:S(2)}) copy-start(pred[128,32]{0,1:T(8,128)(4,1)S(1)} %copy.310) | copy-start | bytes 12292
  34.9 29.7 %collective-permute-start.18 = (bf16[128,32,128]{0,2,1:T(8,128)(2,1)}, bf16[128,32,128]{0,2,1:T(8,128)(2,1)S(1)}, u32[]{:S(2)}, u32[]{:S(2)}) collective-permute-start(bf16[128,32,128]{0,2,1:T(8,128)(2,1)} %get-tuple-element.42), channel_id=1, source_target_pairs={{0,1},{1,0},{2,3},{3,2},{4,5},{5,4},{6,7},{7,6},{8,9},{9,8},{10,11... | collective-permute-start | bytes 3145736 | tf_op jit(solution)/shard_map/ppermute | solution.py:27
  37.1 22.4 %collective-permute-start.39 = (bf16[64,32,128]{2,1,0:T(8,128)(2,1)S(1)}, bf16[64,32,128]{2,1,0:T(8,128)(2,1)S(1)}, u32[]{:S(2)}, u32[]{:S(2)}) collective-permute-start(bf16[64,32,128]{2,1,0:T(8,128)(2,1)S(1)} %maximum_select_fusion.44), channel_id=1, source_target_pairs={{0,2},{2,0},{1,3},{3,1},{4,6},{6,4},{5,7},{7,5},{8,10},{10,8},{9,1... | collective-permute-start | bytes 1572872 | tf_op jit(solution)/shard_map/ppermute | solution.py:27
  48.3 33.6 %collective-permute-start.3 = (bf16[128,32,128]{2,1,0:T(8,128)(2,1)S(1)}, bf16[128,32,128]{2,1,0:T(8,128)(2,1)S(1)}, u32[]{:S(2)}, u32[]{:S(2)}) collective-permute-start(bf16[128,32,128]{2,1,0:T(8,128)(2,1)S(1)} %maximum_select_fusion.24), channel_id=1, source_target_pairs={{0,2},{2,0},{1,3},{3,1},{4,6},{6,4},{5,7},{7,5},{8,10},{10,8},{9,1... | collective-permute-start | bytes 3145736 | tf_op jit(solution)/shard_map/ppermute | solution.py:27
  52.6 51.7 %collective-permute-start.12 = (bf16[128,32,128]{2,1,0:T(8,128)(2,1)S(1)}, bf16[128,32,128]{2,1,0:T(8,128)(2,1)S(1)}, u32[]{:S(2)}, u32[]{:S(2)}) collective-permute-start(bf16[128,32,128]{2,1,0:T(8,128)(2,1)S(1)} %maximum_select_fusion.26), channel_id=1, source_target_pairs={{0,2},{2,0},{1,3},{3,1},{4,6},{6,4},{5,7},{7,5},{8,10},{10,8},{9,1... | collective-permute-start | bytes 3145736 | tf_op jit(solution)/shard_map/ppermute | solution.py:27
  55.4 119.1 %copy-start.29 = (bf16[256,32,128]{0,2,1:T(8,128)(2,1)}, bf16[256,32,128]{0,2,1:T(8,128)(2,1)S(1)}, u32[]{:S(2)}) copy-start(bf16[256,32,128]{0,2,1:T(8,128)(2,1)S(1)} %maximum_select_fusion.12) | copy-start | bytes 6291460
  59.4 67.4 %collective-permute-start.27 = (bf16[128,32,128]{2,1,0:T(8,128)(2,1)S(1)}, bf16[128,32,128]{2,1,0:T(8,128)(2,1)S(1)}, u32[]{:S(2)}, u32[]{:S(2)}) collective-permute-start(bf16[128,32,128]{2,1,0:T(8,128)(2,1)S(1)} %maximum_select_fusion.28), channel_id=1, source_target_pairs={{0,2},{2,0},{1,3},{3,1},{4,6},{6,4},{5,7},{7,5},{8,10},{10,8},{9,1... | collective-permute-start | bytes 3145736 | tf_op jit(solution)/shard_map/ppermute | solution.py:27
  60.7 111.2 %collective-permute-start.1 = (bf16[256,32,128]{0,2,1:T(8,128)(2,1)S(1)}, bf16[256,32,128]{0,2,1:T(8,128)(2,1)S(1)}, u32[]{:S(2)}, u32[]{:S(2)}) collective-permute-start(bf16[256,32,128]{0,2,1:T(8,128)(2,1)S(1)} %maximum_select_fusion.12), channel_id=1, source_target_pairs={{0,2},{2,0},{1,3},{3,1},{4,6},{6,4},{5,7},{7,5},{8,10},{10,8},{9,1... | collective-permute-start | bytes 6291464 | tf_op jit(solution)/shard_map/ppermute | solution.py:27
  62.7 20.5 %copy-start.19 = (bf16[128,32,128]{0,2,1:T(8,128)(2,1)S(1)}, bf16[128,32,128]{0,2,1:T(8,128)(2,1)}, u32[]{:S(2)}) copy-start(bf16[128,32,128]{0,2,1:T(8,128)(2,1)} %get-tuple-element.42) | copy-start | bytes 3145732
  64.6 65.4 %collective-permute-start.16 = (bf16[128,32,128]{2,1,0:T(8,128)(2,1)S(1)}, bf16[128,32,128]{2,1,0:T(8,128)(2,1)S(1)}, u32[]{:S(2)}, u32[]{:S(2)}) collective-permute-start(bf16[128,32,128]{2,1,0:T(8,128)(2,1)S(1)} %maximum_select_fusion.27), channel_id=1, source_target_pairs={{0,4},{4,0},{1,5},{5,1},{2,6},{6,2},{3,7},{7,3},{8,12},{12,8},{9,1... | collective-permute-start | bytes 3145736 | tf_op jit(solution)/shard_map/ppermute | solution.py:27
  81.9 50.0 %collective-permute-start.7 = (bf16[128,32,128]{2,1,0:T(8,128)(2,1)S(1)}, bf16[128,32,128]{2,1,0:T(8,128)(2,1)S(1)}, u32[]{:S(2)}, u32[]{:S(2)}) collective-permute-start(bf16[128,32,128]{2,1,0:T(8,128)(2,1)S(1)} %maximum_select_fusion.25), channel_id=1, source_target_pairs={{0,4},{4,0},{1,5},{5,1},{2,6},{6,2},{3,7},{7,3},{8,12},{12,8},{9,1... | collective-permute-start | bytes 3145736 | tf_op jit(solution)/shard_map/ppermute | solution.py:27
  104.4 30.5 %collective-permute-start.40 = (bf16[128,32,128]{2,1,0:T(8,128)(2,1)S(1)}, bf16[128,32,128]{2,1,0:T(8,128)(2,1)S(1)}, u32[]{:S(2)}, u32[]{:S(2)}) collective-permute-start(bf16[128,32,128]{2,1,0:T(8,128)(2,1)S(1)} %maximum_select_fusion.30), channel_id=1, source_target_pairs={{0,4},{4,0},{1,5},{5,1},{2,6},{6,2},{3,7},{7,3},{8,12},{12,8},{9,1... | collective-permute-start | bytes 3145736 | tf_op jit(solution)/shard_map/ppermute | solution.py:27
  126.8 90.0 %collective-permute-start.19 = (bf16[256,32,128]{0,2,1:T(8,128)(2,1)}, bf16[256,32,128]{0,2,1:T(8,128)(2,1)}, u32[]{:S(2)}, u32[]{:S(2)}) collective-permute-start(bf16[256,32,128]{0,2,1:T(8,128)(2,1)} %maximum_select_fusion.18), channel_id=1, source_target_pairs={{0,2},{2,0},{1,3},{3,1},{4,6},{6,4},{5,7},{7,5},{8,10},{10,8},{9,1... | collective-permute-start | bytes 6291464 | tf_op jit(solution)/shard_map/ppermute | solution.py:27
  130.1 204.0 %collective-permute-start.10 = (bf16[256,32,128]{0,2,1:T(8,128)(2,1)}, bf16[256,32,128]{0,2,1:T(8,128)(2,1)}, u32[]{:S(2)}, u32[]{:S(2)}) collective-permute-start(bf16[256,32,128]{0,2,1:T(8,128)(2,1)} %maximum_select_fusion.15), channel_id=1, source_target_pairs={{0,2},{2,0},{1,3},{3,1},{4,6},{6,4},{5,7},{7,5},{8,10},{10,8},{9,1... | collective-permute-start | bytes 6291464 | tf_op jit(solution)/shard_map/ppermute | solution.py:27
  131.9 94.8 %collective-permute-start.4 = (bf16[256,32,128]{2,1,0:T(8,128)(2,1)}, bf16[256,32,128]{2,1,0:T(8,128)(2,1)}, u32[]{:S(2)}, u32[]{:S(2)}) collective-permute-start(bf16[256,32,128]{2,1,0:T(8,128)(2,1)} %maximum_select_fusion.13), channel_id=1, source_target_pairs={{0,4},{4,0},{1,5},{5,1},{2,6},{6,2},{3,7},{7,3},{8,12},{12,8},{9,1... | collective-permute-start | bytes 6291464 | tf_op jit(solution)/shard_map/ppermute | solution.py:27
  134.9 101.0 %collective-permute-start.13 = (bf16[256,32,128]{2,1,0:T(8,128)(2,1)S(1)}, bf16[256,32,128]{2,1,0:T(8,128)(2,1)}, u32[]{:S(2)}, u32[]{:S(2)}) collective-permute-start(bf16[256,32,128]{2,1,0:T(8,128)(2,1)S(1)} %maximum_select_fusion.16), channel_id=1, source_target_pairs={{0,4},{4,0},{1,5},{5,1},{2,6},{6,2},{3,7},{7,3},{8,12},{12,8},{9,1... | collective-permute-start | bytes 6291464 | tf_op jit(solution)/shard_map/ppermute | solution.py:27
  173.2 94.7 %collective-permute-start.28 = (bf16[256,32,128]{2,1,0:T(8,128)(2,1)}, bf16[256,32,128]{2,1,0:T(8,128)(2,1)}, u32[]{:S(2)}, u32[]{:S(2)}) collective-permute-start(bf16[256,32,128]{2,1,0:T(8,128)(2,1)} %maximum_select_fusion.20), channel_id=1, source_target_pairs={{0,4},{4,0},{1,5},{5,1},{2,6},{6,2},{3,7},{7,3},{8,12},{12,8},{9,1... | collective-permute-start | bytes 6291464 | tf_op jit(solution)/shard_map/ppermute | solution.py:27
  216.8 101.5 %collective-permute-start.17 = (bf16[256,32,128]{2,1,0:T(8,128)(2,1)}, bf16[256,32,128]{2,1,0:T(8,128)(2,1)}, u32[]{:S(2)}, u32[]{:S(2)}) collective-permute-start(bf16[256,32,128]{2,1,0:T(8,128)(2,1)} %maximum_select_fusion.17), channel_id=1, source_target_pairs={{0,8},{8,0},{1,9},{9,1},{2,10},{10,2},{3,11},{11,3},{4,12},{12,4},... | collective-permute-start | bytes 6291464 | tf_op jit(solution)/shard_map/ppermute | solution.py:27
  226.8 81.7 %collective-permute-start.8 = (bf16[256,32,128]{2,1,0:T(8,128)(2,1)}, bf16[256,32,128]{2,1,0:T(8,128)(2,1)}, u32[]{:S(2)}, u32[]{:S(2)}) collective-permute-start(bf16[256,32,128]{2,1,0:T(8,128)(2,1)} %maximum_select_fusion.14), channel_id=1, source_target_pairs={{0,8},{8,0},{1,9},{9,1},{2,10},{10,2},{3,11},{11,3},{4,12},{12,4},... | collective-permute-start | bytes 6291464 | tf_op jit(solution)/shard_map/ppermute | solution.py:27
  235.9 209.5 %collective-permute-start.41 = (bf16[256,32,128]{2,1,0:T(8,128)(2,1)}, bf16[256,32,128]{2,1,0:T(8,128)(2,1)}, u32[]{:S(2)}, u32[]{:S(2)}) collective-permute-start(bf16[256,32,128]{2,1,0:T(8,128)(2,1)} %maximum_select_fusion.22), channel_id=1, source_target_pairs={{0,8},{8,0},{1,9},{9,1},{2,10},{10,2},{3,11},{11,3},{4,12},{12,4},... | collective-permute-start | bytes 6291464 | tf_op jit(solution)/shard_map/ppermute | solution.py:27
  407.3 72.6 %collective-permute-start.42 = (f32[32,32]{1,0:T(8,128)}, f32[32,32]{1,0:T(8,128)}, u32[]{:S(2)}, u32[]{:S(2)}) collective-permute-start(f32[32,32]{1,0:T(8,128)} %get-tuple-element.10), channel_id=1, source_target_pairs={{0,1},{1,0},{2,3},{3,2},{4,5},{5,4},{6,7},{7,6},{8,9},{9,8},{10,11... | collective-permute-start | bytes 12296 | tf_op jit(solution)/shard_map/ppermute | solution.py:27
  411.0 68.0 %collective-permute-start.50 = (f32[32,32]{1,0:T(8,128)}, f32[32,32]{1,0:T(8,128)}, u32[]{:S(2)}, u32[]{:S(2)}) collective-permute-start(f32[32,32]{1,0:T(8,128)} %get-tuple-element.11), channel_id=1, source_target_pairs={{0,1},{1,0},{2,3},{3,2},{4,5},{5,4},{6,7},{7,6},{8,9},{9,8},{10,11... | collective-permute-start | bytes 12296 | tf_op jit(solution)/shard_map/ppermute | solution.py:27
  413.2 87.2 %collective-permute-start.32 = (bf16[64,32,128]{2,1,0:T(8,128)(2,1)}, bf16[64,32,128]{2,1,0:T(8,128)(2,1)}, u32[]{:S(2)}, u32[]{:S(2)}) collective-permute-start(bf16[64,32,128]{2,1,0:T(8,128)(2,1)} %select_reduce_fusion.1), channel_id=1, source_target_pairs={{0,1},{1,0},{2,3},{3,2},{4,5},{5,4},{6,7},{7,6},{8,9},{9,8},{10,11... | collective-permute-start | bytes 1572872 | tf_op jit(solution)/shard_map/ppermute | solution.py:27
  413.7 80.3 %collective-permute-start.46 = (bf16[32,32,128]{2,1,0:T(8,128)(2,1)}, bf16[32,32,128]{2,1,0:T(8,128)(2,1)}, u32[]{:S(2)}, u32[]{:S(2)}) collective-permute-start(bf16[32,32,128]{2,1,0:T(8,128)(2,1)} %select_reduce_fusion), channel_id=1, source_target_pairs={{0,1},{1,0},{2,3},{3,2},{4,5},{5,4},{6,7},{7,6},{8,9},{9,8},{10,11... | collective-permute-start | bytes 786440 | tf_op jit(solution)/shard_map/ppermute | solution.py:27
  445.4 44.6 %collective-permute-start.22 = (bf16[128,32,128]{0,2,1:T(8,128)(2,1)S(1)}, bf16[128,32,128]{0,2,1:T(8,128)(2,1)}, u32[]{:S(2)}, u32[]{:S(2)}) collective-permute-start(bf16[128,32,128]{0,2,1:T(8,128)(2,1)S(1)} %copy-done.20), channel_id=1, source_target_pairs={{0,1},{1,0},{2,3},{3,2},{4,5},{5,4},{6,7},{7,6},{8,9},{9,8},{10,11... | collective-permute-start | bytes 3145736 | tf_op jit(solution)/shard_map/ppermute | solution.py:27
  474.0 20.1 %copy-start.32 = (bf16[32,32,128]{2,1,0:T(8,128)(2,1)S(1)}, bf16[32,32,128]{2,1,0:T(8,128)(2,1)}, u32[]{:S(2)}) copy-start(bf16[32,32,128]{2,1,0:T(8,128)(2,1)} %select_reduce_fusion) | copy-start | bytes 786436
  479.0 2.3 collective-permute-start.35
  479.9 4.0 collective-permute-start.29
  481.4 6.2 collective-permute-start.51
  483.9 4.8 collective-permute-start.43
  487.6 8.1 %collective-permute-start.24 = (f32[128,32]{0,1:T(8,128)}, f32[128,32]{0,1:T(8,128)}, u32[]{:S(2)}, u32[]{:S(2)}) collective-permute-start(f32[128,32]{0,1:T(8,128)} %broadcast_select_fusion.8), channel_id=1, source_target_pairs={{0,1},{1,0},{2,3},{3,2},{4,5},{5,4},{6,7},{7,6},{8,9},{9,8},{10,11... | collective-permute-start | bytes 49160 | tf_op jit(solution)/shard_map/ppermute | solution.py:27
  488.8 8.9 %collective-permute-start.20 = (f32[128,32]{0,1:T(8,128)}, f32[128,32]{0,1:T(8,128)}, u32[]{:S(2)}, u32[]{:S(2)}) collective-permute-start(f32[128,32]{0,1:T(8,128)} %get-tuple-element.18), channel_id=1, source_target_pairs={{0,1},{1,0},{2,3},{3,2},{4,5},{5,4},{6,7},{7,6},{8,9},{9,8},{10,11... | collective-permute-start | bytes 49160 | tf_op jit(solution)/shard_map/ppermute | solution.py:27
  490.0 8.9 %collective-permute-start.36 = (f32[128,32]{0,1:T(8,128)}, f32[128,32]{0,1:T(8,128)S(1)}, u32[]{:S(2)}, u32[]{:S(2)}) collective-permute-start(f32[128,32]{0,1:T(8,128)} %maximum_select_fusion.61), channel_id=1, source_target_pairs={{0,2},{2,0},{1,3},{3,1},{4,6},{6,4},{5,7},{7,5},{8,10},{10,8},{9,1... | collective-permute-start | bytes 49160 | tf_op jit(solution)/shard_map/ppermute | solution.py:27
  494.0 91.3 %copy-start.31 = (bf16[256,32,128]{0,2,1:T(8,128)(2,1)}, bf16[256,32,128]{0,2,1:T(8,128)(2,1)S(1)}, u32[]{:S(2)}) copy-start(bf16[256,32,128]{0,2,1:T(8,128)(2,1)S(1)} %maximum_select_fusion.19) | copy-start | bytes 6291460
  494.1 94.5 %collective-permute-start.23 = (bf16[256,32,128]{0,2,1:T(8,128)(2,1)S(1)}, bf16[256,32,128]{0,2,1:T(8,128)(2,1)}, u32[]{:S(2)}, u32[]{:S(2)}) collective-permute-start(bf16[256,32,128]{0,2,1:T(8,128)(2,1)S(1)} %maximum_select_fusion.19), channel_id=1, source_target_pairs={{0,2},{2,0},{1,3},{3,1},{4,6},{6,4},{5,7},{7,5},{8,10},{10,8},{9,1... | collective-permute-start | bytes 6291464 | tf_op jit(solution)/shard_map/ppermute | solution.py:27
  495.7 56.7 %collective-permute-start.47 = (bf16[64,32,128]{2,1,0:T(8,128)(2,1)S(1)}, bf16[64,32,128]{2,1,0:T(8,128)(2,1)S(1)}, u32[]{:S(2)}, u32[]{:S(2)}) collective-permute-start(bf16[64,32,128]{2,1,0:T(8,128)(2,1)S(1)} %maximum_select_fusion.45), channel_id=1, source_target_pairs={{0,2},{2,0},{1,3},{3,1},{4,6},{6,4},{5,7},{7,5},{8,10},{10,8},{9,1... | collective-permute-start | bytes 1572872 | tf_op jit(solution)/shard_map/ppermute | solution.py:27
  497.6 54.4 %collective-permute-start.30 = (f32[128,32]{0,1:T(8,128)S(1)}, f32[128,32]{0,1:T(8,128)S(1)}, u32[]{:S(2)}, u32[]{:S(2)}) collective-permute-start(f32[128,32]{0,1:T(8,128)S(1)} %copy-done.53), channel_id=1, source_target_pairs={{0,2},{2,0},{1,3},{3,1},{4,6},{6,4},{5,7},{7,5},{8,10},{10,8},{9,1... | collective-permute-start | bytes 49160 | tf_op jit(solution)/shard_map/ppermute | solution.py:27
  498.9 54.9 %collective-permute-start.52 = (f32[128,32]{0,1:T(8,128)S(1)}, f32[128,32]{0,1:T(8,128)S(1)}, u32[]{:S(2)}, u32[]{:S(2)}) collective-permute-start(f32[128,32]{0,1:T(8,128)S(1)} %maximum_select_fusion.63), channel_id=1, source_target_pairs={{0,4},{4,0},{1,5},{5,1},{2,6},{6,2},{3,7},{7,3},{8,12},{12,8},{9,1... | collective-permute-start | bytes 49160 | tf_op jit(solution)/shard_map/ppermute | solution.py:27
  500.4 54.7 %collective-permute-start.44 = (f32[128,32]{0,1:T(8,128)S(1)}, f32[128,32]{0,1:T(8,128)S(1)}, u32[]{:S(2)}, u32[]{:S(2)}) collective-permute-start(f32[128,32]{0,1:T(8,128)S(1)} %maximum_select_fusion.62), channel_id=1, source_target_pairs={{0,4},{4,0},{1,5},{5,1},{2,6},{6,2},{3,7},{7,3},{8,12},{12,8},{9,1... | collective-permute-start | bytes 49160 | tf_op jit(solution)/shard_map/ppermute | solution.py:27
  552.1 31.6 %collective-permute-start.33 = (bf16[128,32,128]{2,1,0:T(8,128)(2,1)S(1)}, bf16[128,32,128]{2,1,0:T(8,128)(2,1)S(1)}, u32[]{:S(2)}, u32[]{:S(2)}) collective-permute-start(bf16[128,32,128]{2,1,0:T(8,128)(2,1)S(1)} %maximum_select_fusion.29), channel_id=1, source_target_pairs={{0,2},{2,0},{1,3},{3,1},{4,6},{6,4},{5,7},{7,5},{8,10},{10,8},{9,1... | collective-permute-start | bytes 3145736 | tf_op jit(solution)/shard_map/ppermute | solution.py:27
  552.4 23.4 %collective-permute-start.25 = (f32[256,32]{0,1:T(8,128)S(1)}, f32[256,32]{0,1:T(8,128)S(1)}, u32[]{:S(2)}, u32[]{:S(2)}) collective-permute-start(f32[256,32]{0,1:T(8,128)S(1)} %maximum_select_fusion.53), channel_id=1, source_target_pairs={{0,2},{2,0},{1,3},{3,1},{4,6},{6,4},{5,7},{7,5},{8,10},{10,8},{9,1... | collective-permute-start | bytes 98312 | tf_op jit(solution)/shard_map/ppermute | solution.py:27
  553.8 32.5 %collective-permute-start.48 = (bf16[128,32,128]{2,1,0:T(8,128)(2,1)S(1)}, bf16[128,32,128]{2,1,0:T(8,128)(2,1)S(1)}, u32[]{:S(2)}, u32[]{:S(2)}) collective-permute-start(bf16[128,32,128]{2,1,0:T(8,128)(2,1)S(1)} %maximum_select_fusion.31), channel_id=1, source_target_pairs={{0,4},{4,0},{1,5},{5,1},{2,6},{6,2},{3,7},{7,3},{8,12},{12,8},{9,1... | collective-permute-start | bytes 3145736 | tf_op jit(solution)/shard_map/ppermute | solution.py:27
  555.1 21.9 %collective-permute-start.21 = (f32[256,32]{0,1:T(8,128)S(1)}, f32[256,32]{0,1:T(8,128)S(1)}, u32[]{:S(2)}, u32[]{:S(2)}) collective-permute-start(f32[256,32]{0,1:T(8,128)S(1)} %maximum_select_fusion.52), channel_id=1, source_target_pairs={{0,2},{2,0},{1,3},{3,1},{4,6},{6,4},{5,7},{7,5},{8,10},{10,8},{9,1... | collective-permute-start | bytes 98312 | tf_op jit(solution)/shard_map/ppermute | solution.py:27
  575.8 3.5 collective-permute-start.37
  577.0 3.5 collective-permute-start.31
  579.3 3.0 collective-permute-start.53
  580.6 3.1 collective-permute-start.45
  585.4 42.9 %collective-permute-start.34 = (bf16[256,32,128]{2,1,0:T(8,128)(2,1)}, bf16[256,32,128]{2,1,0:T(8,128)(2,1)}, u32[]{:S(2)}, u32[]{:S(2)}) collective-permute-start(bf16[256,32,128]{2,1,0:T(8,128)(2,1)} %maximum_select_fusion.21), channel_id=1, source_target_pairs={{0,4},{4,0},{1,5},{5,1},{2,6},{6,2},{3,7},{7,3},{8,12},{12,8},{9,1... | collective-permute-start | bytes 6291464 | tf_op jit(solution)/shard_map/ppermute | solution.py:27
  588.0 71.5 %collective-permute-start.49 = (bf16[256,32,128]{2,1,0:T(8,128)(2,1)}, bf16[256,32,128]{2,1,0:T(8,128)(2,1)}, u32[]{:S(2)}, u32[]{:S(2)}) collective-permute-start(bf16[256,32,128]{2,1,0:T(8,128)(2,1)} %maximum_select_fusion.23), channel_id=1, source_target_pairs={{0,8},{8,0},{1,9},{9,1},{2,10},{10,2},{3,11},{11,3},{4,12},{12,4},... | collective-permute-start | bytes 6291464 | tf_op jit(solution)/shard_map/ppermute | solution.py:27
  (58 other events, 407.0 us)
where the time goes:
time: 717 us; the launch traced here: 706 us
  waiting for transfers between devices  262 us (37%)
  matrix products  164 us (23%)
  other arithmetic  133 us (19%)
  local copies, waits for them, and re-layouts  104 us (15%)
  starting transfers between devices  40.8 us (6%)
    ppermute x54, waiting for transfers between devices, from_partner(): return lax.ppermute(block, axis, route)  262 us
    select_n x44, other arithmetic, doubling(): jnp.where(is_lower, jnp.concatenate([own_part, peer_part], 0), jnp.concat...  78.7 us
    dot_general x3, matrix products, grad_block(): jnp.einsum('shqk,sqhd->skhd', dscores, query_seg, preferred_element_type=...  41.9 us
    ppermute x54, starting transfers between devices, from_partner(): return lax.ppermute(block, axis, route)  40.8 us
    dot_general x3, matrix products, grad_block(): jnp.einsum('shqk,skhd->sqhd', dscores, key_seg, preferred_element_type=jn...  40.3 us
    broadcast_in_dim x39, local copies, waits for them, and re-layouts, put_rows(): jnp.where(chosen, picked[:, None], jnp.asarray(filler, picked.dtype))  29 us
    dot_general x3, matrix products, grad_block(): jnp.einsum('sqhd,skhd->shqk', query_seg, key_seg, preferred_element_type=...  23.2 us
    dot_general x3, matrix products, grad_block(): jnp.einsum('shqk,sqhd->skhd', probs_half, dout_seg, preferred_element_typ...  22.1 us
  transfers between devices with their start and end apart: 54, of which 16 were waited for; matrix products, arithmetic and copies ran while one was open for 49% of the time, Pallas kernels for 0%

commit v1 on v0

v1 whole, which is shorter than its diff:
```python
import functools
import math

import jax
import jax.numpy as jnp
from jax import lax
from jax.experimental import pallas as pl
from jax.experimental.pallas import tpu as pltpu
from jax.sharding import PartitionSpec as P

SEG0 = 512
LEVELS = 3
HD = 128
RES = 2 ** (LEVELS - 1)
NEG_FILL = -1e30
EPSILON = 1e-05
LOG2E = math.log2(math.e)
SCALE = 1.0 / math.sqrt(HD)
F32 = jnp.float32
BF16 = jnp.bfloat16


def nn(a, b):
    return lax.dot_general(a, b, (((1,), (0,)), ((), ())), preferred_element_type=F32)


def nt(a, b):
    return lax.dot_general(a, b, (((1,), (1,)), ((), ())), preferred_element_type=F32)


def wait_bytes(ref, sem):
    pltpu.make_async_copy(ref, ref, sem).wait()


def kernel(
    G, NH, HPD, T, total_features,
    offs, gain, q_in, k_in, v_in, c_in,
    n_out, dq_out, dk_out, dv_out,
    stage, recv, recv_c, osta, rout, kT, vT, attT, doT, doN,
    o1, ml1, o2, ml2, dq1, dk1, dv1, dq2, dk2, dv2,
    lse, delta, srecv, tot,
    send_sem, recv_sem, osend_sem, orecv_sem, ssend_sem, srecv_sem,
):
    R = T // RES
    LEN = G * R
    NP = G * NH
    SRC0 = SEG0 // T
    W0 = SRC0 * R
    SEGS0 = G // SRC0
    ctx = lax.axis_index("ctx")
    hidx = lax.axis_index("head")
    mine = lax.rem(ctx, G)
    base = ctx - mine
    slot = hidx * G + mine

    barrier = pltpu.get_barrier_semaphore()

    def greet(i, c):
        peer = lax.rem(slot + i, NP)
        pl.semaphore_signal(
            barrier, inc=1,
            device_id={"ctx": base + lax.rem(peer, G), "head": peer // G},
            device_id_type=pl.DeviceIdType.MESH,
        )
        return c

    lax.fori_loop(1, NP, greet, 0)

    ia = lax.broadcasted_iota(jnp.int32, (T, T), 0)
    ib = lax.broadcasted_iota(jnp.int32, (T, T), 1)
    perm = jnp.where(ib == lax.rem(ia, R) * RES + ia // R, 1.0, 0.0).astype(BF16)
    perm_t = jnp.where(ia == lax.rem(ib, R) * RES + ib // R, 1.0, 0.0).astype(BF16)
    ja = lax.broadcasted_iota(jnp.int32, (HD, HD), 0)
    jb = lax.broadcasted_iota(jnp.int32, (HD, HD), 1)
    eye_mask = ja == jb
    eye = jnp.where(eye_mask, 1.0, 0.0).astype(BF16)

    F = HPD * HD

    def put_stage(a, ref):
        for d in range(G):
            y = nn(perm, ref[:, d * F:(d + 1) * F]).astype(BF16)
            for hh in range(HPD):
                stage[a, d, hh] = y[:, hh * HD:(hh + 1) * HD].reshape(RES, R, HD)

    def send_stage(a):
        into = recv.at[a] if a < 3 else recv_c

        def one(i, c):
            d = lax.rem(mine + i, G)
            pltpu.make_async_remote_copy(
                src_ref=stage.at[a, d],
                dst_ref=into.at[:, :, mine],
                send_sem=send_sem.at[a],
                recv_sem=recv_sem.at[a],
                device_id={"ctx": base + d},
                device_id_type=pl.DeviceIdType.MESH,
            ).start()
            return c

        lax.fori_loop(1, G, one, 0)
        into[:, :, mine] = stage[a, mine]

    put_stage(0, q_in)
    pl.semaphore_wait(barrier, NP - 1)
    send_stage(0)
    for a, ref in ((1, k_in), (2, v_in), (3, c_in)):
        put_stage(a, ref)
        send_stage(a)

    def offset(level, hh):
        if level == 0:
            return 0
        return offs[level, mine * HPD + hh]

    def n_pick(load, level, s, off):
        n = SRC0 << level
        parts = [
            load(off + (j << level), pl.ds(s * n, n)).reshape(n * R, HD)
            for j in range(RES >> level)
        ]
        return parts[0] if len(parts) == 1 else jnp.concatenate(parts, 0)

    def t_pick(load, level, s, off):
        w = W0 << level
        start = s * w if isinstance(s, int) else pl.multiple_of(s * w, w)
        parts = [load(off + (j << level), pl.ds(start, w)) for j in range(RES >> level)]
        return parts[0] if len(parts) == 1 else jnp.concatenate(parts, 1)

    for a in range(3):
        wait_bytes(recv.at[a, :, :, pl.ds(0, G - 1)], recv_sem.at[a])

    def rows(a, hh):
        return lambda r, d: recv[a, hh, r, d]

    def turn(x):
        return nt(eye, x).astype(BF16)

    def level1_at(s, r):
        return pl.multiple_of((r // 2) * (2 * W0) + lax.rem(s, 2) * W0, W0)

    def forward(hh, carry):
        for r in range(RES):
            kT[hh, r] = turn(recv[1, hh, r].reshape(LEN, HD))
            vT[r] = turn(recv[2, hh, r].reshape(LEN, HD))
        offsets = [offset(level, hh) for level in range(LEVELS)]

        def segment(level, s):
            off = offsets[level]
            qn = n_pick(rows(0, hh), level, s, off)
            kn = n_pick(rows(1, hh), level, s, off)
            vt = t_pick(lambda r, d: vT[r, :, d], level, s, off)
            st = nt(kn, qn) * (SCALE * LOG2E)
            top = jnp.max(st, axis=0, keepdims=True)
            p = jnp.exp2(st - top)
            return nn(vt, p.astype(BF16)), top, jnp.sum(p, axis=0, keepdims=True)

        o, m, l = segment(2, 0)
        o2[...] = o
        ml2[0] = m
        ml2[1] = l
        for s in range(2):
            o, m, l = segment(1, s)
            o1[s] = o
            ml1[s, 0] = m
            ml1[s, 1] = l

        def level0(s, c):
            o, m, l = segment(0, s)
            lanes2 = pl.ds(pl.multiple_of(s * W0, W0), W0)
            for r in range(RES):
                here = slice(r * W0, (r + 1) * W0)
                lanes1 = pl.ds(level1_at(s, r), W0)
                m0 = m[:, here]
                m1 = jnp.where(offsets[1] == r % 2, ml1[s // 2, 0, :, lanes1], NEG_FILL)
                m2 = jnp.where(offsets[2] == r, ml2[0, :, lanes2], NEG_FILL)
                top = jnp.maximum(m0, jnp.maximum(m1, m2))
                f0 = jnp.exp2(m0 - top)
                f1 = jnp.exp2(m1 - top)
                f2 = jnp.exp2(m2 - top)
                total = f0 * l[:, here] + f1 * ml1[s // 2, 1, :, lanes1] + f2 * ml2[1, :, lanes2]
                summed = f0 * o[:, here] + f1 * o1[s // 2, :, lanes1] + f2 * o2[:, lanes2]
                attT[hh, r, :, lanes2] = (summed / total).astype(BF16)
                lse[hh, r, :, lanes2] = top + jnp.log(total) * LOG2E
            return c

        lax.fori_loop(0, SEGS0, level0, 0)
        return carry

    lax.fori_loop(0, HPD, forward, 0)

    wait_bytes(recv_c.at[:, :, pl.ds(0, G - 1)], recv_sem.at[3])

    def gain_of(hh):
        g = gain[pl.ds(mine * HPD + hh, 1), :]
        return jnp.sum(jnp.where(eye_mask, g, 0.0), axis=1, keepdims=True)

    gains = [gain_of(hh) for hh in range(HPD)]
    for r in range(RES):
        sums = None
        for hh in range(HPD):
            a = attT[hh, r].astype(F32)
            cT = turn(recv_c[hh, r].reshape(LEN, HD))
            doT[hh, r] = cT
            dx = cT.astype(F32) * gains[hh]
            part = [jnp.sum(x, axis=0, keepdims=True) for x in (a, a * a, dx, dx * a)]
            sums = part if sums is None else [x + y for x, y in zip(sums, part)]
        for kind in range(4):
            srecv[slot, kind * RES + r] = sums[kind]

    def send_stats(i, c):
        peer = lax.rem(slot + i, NP)
        pltpu.make_async_remote_copy(
            src_ref=srecv.at[slot],
            dst_ref=srecv.at[slot],
            send_sem=ssend_sem,
            recv_sem=srecv_sem,
            device_id={"ctx": base + lax.rem(peer, G), "head": peer // G},
            device_id_type=pl.DeviceIdType.MESH,
        ).start()
        return c

    lax.fori_loop(1, NP, send_stats, 0)
    wait_bytes(srecv.at[pl.ds(0, NP - 1)], srecv_sem)
    tot[...] = jnp.sum(srecv[...], axis=0)

    inv_f = 1.0 / total_features
    for r in range(RES):
        mean = tot[r] * inv_f
        var = tot[RES + r] * inv_f - mean * mean
        inv = 1.0 / jnp.sqrt(var + EPSILON)
        s1 = tot[2 * RES + r]
        s2 = inv * (tot[3 * RES + r] - mean * s1)
        s1 = s1 * inv_f
        s2 = s2 * inv_f
        for hh in range(HPD):
            a = attT[hh, r].astype(F32)
            xhat = (a - mean) * inv
            normed = (xhat * gains[hh]).astype(BF16)
            dx = doT[hh, r].astype(F32) * gains[hh]
            d = ((dx - s1 - xhat * s2) * inv).astype(BF16)
            delta[hh, r] = jnp.sum(d.astype(F32) * a, axis=0, keepdims=True)
            doT[hh, r] = d
            n = SRC0
            for s in range(SEGS0):
                here = slice(s * W0, (s + 1) * W0)
                osta[0, hh, r, s * n:(s + 1) * n] = turn(normed[:, here]).reshape(n, R, HD)
                doN[hh, r, s * n:(s + 1) * n] = turn(d[:, here]).reshape(n, R, HD)

    def send_normed(i, c):
        d = lax.rem(mine + i, G)
        pltpu.make_async_remote_copy(
            src_ref=osta.at[0, :, :, d],
            dst_ref=rout.at[0, :, mine],
            send_sem=osend_sem.at[0],
            recv_sem=orecv_sem.at[0],
            device_id={"ctx": base + d},
            device_id_type=pl.DeviceIdType.MESH,
        ).start()
        return c

    lax.fori_loop(1, G, send_normed, 0)
    rout[0, :, mine] = osta[0, :, :, mine]

    def backward(hh, carry):
        offsets = [offset(level, hh) for level in range(LEVELS)]

        def segment(level, s):
            off = offsets[level]
            qn = n_pick(rows(0, hh), level, s, off)
            kn = n_pick(rows(1, hh), level, s, off)
            vn = n_pick(rows(2, hh), level, s, off)
            dn = n_pick(lambda r, d: doN[hh, r, d], level, s, off)
            dt = t_pick(lambda r, d: doT[hh, r, :, d], level, s, off)
            kt = t_pick(lambda r, d: kT[hh, r, :, d], level, s, off)
            ls = t_pick(lambda r, d: lse[hh, r, :, d], level, s, off)
            de = t_pick(lambda r, d: delta[hh, r, :, d], level, s, off)
            p = jnp.exp2(nt(kn, qn) * (SCALE * LOG2E) - ls)
            ds = (p * (nn(vn, dt) - de)).astype(BF16)
            return nn(kt, ds), nn(ds, qn), nn(p.astype(BF16), dn)

        dq2[...], dk2[...], dv2[...] = segment(2, 0)
        for s in range(2):
            dq1[s], dk1[s], dv1[s] = segment(1, s)
        w1 = [jnp.where(offsets[1] == r % 2, 1.0, 0.0).astype(F32) for r in range(RES)]
        w2 = [jnp.where(offsets[2] == r, 1.0, 0.0).astype(F32) for r in range(RES)]

        def level0(i, c):
            s = lax.rem(mine // SRC0 + i, SEGS0)
            dq, dk, dv = segment(0, s)
            at2 = pl.ds(pl.multiple_of(s * W0, W0), W0)
            to = pl.ds(s * SRC0, SRC0)
            for r in range(RES):
                here = slice(r * W0, (r + 1) * W0)
                at1 = pl.ds(level1_at(s, r), W0)
                x = (dq[:, here] + w1[r] * dq1[s // 2, :, at1] + w2[r] * dq2[:, at2]) * SCALE
                osta[1, hh, r, to] = turn(x.astype(BF16)).reshape(SRC0, R, HD)
                x = (dk[here] + w1[r] * dk1[s // 2, at1] + w2[r] * dk2[at2]) * SCALE
                osta[2, hh, r, to] = x.astype(BF16).reshape(SRC0, R, HD)
                x = dv[here] + w1[r] * dv1[s // 2, at1] + w2[r] * dv2[at2]
                osta[3, hh, r, to] = x.astype(BF16).reshape(SRC0, R, HD)
            for j in range(SRC0):
                d = s * SRC0 + j

                @pl.when(d != mine)
                def _():
                    pltpu.make_async_remote_copy(
                        src_ref=osta.at[pl.ds(1, 3), hh, :, d],
                        dst_ref=rout.at[pl.ds(1, 3), hh, mine],
                        send_sem=osend_sem.at[1 + hh],
                        recv_sem=orecv_sem.at[1 + hh],
                        device_id={"ctx": base + d},
                        device_id_type=pl.DeviceIdType.MESH,
                    ).start()

            return c

        lax.fori_loop(0, SEGS0, level0, 0)
        rout[pl.ds(1, 3), hh, mine] = osta[pl.ds(1, 3), hh, :, mine]
        return carry

    lax.fori_loop(0, HPD, backward, 0)

    def unpermute(ref, a, hh):
        for g in range(G):
            head = g * HPD + hh
            x = nn(perm_t, rout[a, hh, g].reshape(T, HD))
            ref[:, head * HD:(head + 1) * HD] = x.astype(BF16)

    wait_bytes(rout.at[0, :, pl.ds(0, G - 1)], orecv_sem.at[0])
    for hh in range(HPD):
        unpermute(n_out, 0, hh)
    for hh in range(HPD):
        wait_bytes(rout.at[pl.ds(1, 3), hh, pl.ds(0, G - 1)], orecv_sem.at[1 + hh])
        for a, ref in ((1, dq_out), (2, dk_out), (3, dv_out)):
            unpermute(ref, a, hh)

    for a in range(4):
        wait_bytes(stage.at[a, pl.ds(0, G - 1)], send_sem.at[a])
    wait_bytes(srecv.at[pl.ds(0, NP - 1)], ssend_sem)
    wait_bytes(osta.at[0, :, :, pl.ds(0, G - 1)], osend_sem.at[0])
    for hh in range(HPD):
        wait_bytes(osta.at[pl.ds(1, 3), hh, :, pl.ds(0, G - 1)], osend_sem.at[1 + hh])


def on_device(queries, key_rows, value_rows, offsets, sublayer_norm_gain, cotangent):
    T, features = queries.shape
    heads = offsets.shape[1]
    NH = lax.axis_size("head")
    G = SEG0 * RES // T
    HPD = heads // G
    R = T // RES
    LEN = G * R
    NP = G * NH
    vm = pl.BlockSpec(memory_space=pltpu.VMEM)
    out = jax.ShapeDtypeStruct((T, features), BF16)
    big = pltpu.VMEM((4, HPD, RES, G, R, HD), BF16)
    scratch = [
        pltpu.VMEM((4, G, HPD, RES, R, HD), BF16),
        pltpu.VMEM((3, HPD, RES, G, R, HD), BF16),
        pltpu.VMEM((HPD, RES, G, R, HD), BF16),
        big,
        pltpu.VMEM((4, HPD, G, RES, R, HD), BF16),
        pltpu.VMEM((HPD, RES, HD, LEN), BF16),
        pltpu.VMEM((RES, HD, LEN), BF16),
        pltpu.VMEM((HPD, RES, HD, LEN), BF16),
        pltpu.VMEM((HPD, RES, HD, LEN), BF16),
        pltpu.VMEM((HPD, RES, G, R, HD), BF16),
        pltpu.VMEM((2, HD, SEG0), F32),
        pltpu.VMEM((2, 2, 1, SEG0), F32),
        pltpu.VMEM((HD, SEG0), F32),
        pltpu.VMEM((2, 1, SEG0), F32),
        pltpu.VMEM((2, HD, SEG0), F32),
        pltpu.VMEM((2, SEG0, HD), F32),
        pltpu.VMEM((2, SEG0, HD), F32),
        pltpu.VMEM((HD, SEG0), F32),
        pltpu.VMEM((SEG0, HD), F32),
        pltpu.VMEM((SEG0, HD), F32),
        pltpu.VMEM((HPD, RES, 1, LEN), F32),
        pltpu.VMEM((HPD, RES, 1, LEN), F32),
        pltpu.VMEM((NP, 4 * RES, 1, LEN), F32),
        pltpu.VMEM((4 * RES, 1, LEN), F32),
        pltpu.SemaphoreType.DMA((4,)),
        pltpu.SemaphoreType.DMA((4,)),
        pltpu.SemaphoreType.DMA((1 + HPD,)),
        pltpu.SemaphoreType.DMA((1 + HPD,)),
        pltpu.SemaphoreType.DMA,
        pltpu.SemaphoreType.DMA,
    ]
    return pl.pallas_call(
        functools.partial(kernel, G, NH, HPD, T, float(NH * features)),
        out_shape=(out,) * 4,
        in_specs=[pl.BlockSpec(memory_space=pltpu.SMEM)] + [vm] * 5,
        out_specs=(vm,) * 4,
        scratch_shapes=scratch,
        compiler_params=pltpu.CompilerParams(
            collective_id=0, has_side_effects=True, vmem_limit_bytes=58 * 2**20
        ),
        cost_estimate=pl.CostEstimate(
            flops=7_000_000_000, bytes_accessed=8 * 2**20, transcendentals=8_000_000
        ),
    )(offsets, sublayer_norm_gain.reshape(heads, HD), queries, key_rows, value_rows, cotangent)


def solution(mesh):
    spec = P("ctx", "head")
    return jax.shard_map(
        on_device,
        mesh=mesh,
        in_specs=(spec, spec, spec, P(None, "head"), P("head"), spec),
        out_specs=(spec,) * 4,
        check_vma=False,
    )
```

time: 717 us -> 138 us (0.19)
  the two profiles are of different devices: /device:TPU:1 before, /device:TPU:7 now
where the time goes in v1:
time: 138 us; the launch traced here: 137 us
  Pallas kernels  130 us (94%)
  local copies, waits for them, and re-layouts  6.55 us (5%)
    pallas_call x1, Pallas kernels, on_device(): pl.pallas_call(functools.partial(kernel, G, NH, HPD, T, float(NH * featur...  130 us
    unnamed x10, local copies, waits for them, and re-layouts  6.55 us

profile of v1, /device:TPU:7, one launch (start us, length us, event | category | flops | bytes accessed | tf_op | source)
XLA Modules:
  0.0 137.5 jit_solution(6092148571748900167)
XLA Ops:
  0.6 130.3 %shard_map.93 = (bf16[128,4096]{1,0:T(8,128)(2,1)}, bf16[128,4096]{1,0:T(8,128)(2,1)}, bf16[128,4096]{1,0:T(8,128)(2,1)}, bf16[128,4096]{1,0:T(8,128)(2,1)}) custom-call(s32[3,32]{1,0:T(4,128)} %offs.1, f32[32,128]{1,0:T(8,128)} %bitcast.1, bf16[128,4096]{1,0:T(8,128)(2,1)} %q_in.1, bf16[128,4096]{1,0:T(8,128)(2,1)} %k_in.1, bf16[128,4096]{1,0:T(8,128)(2,1)} %v_in.1, ...), custom_call_target="tpu_custom_call" | custom-call | flops 7000000000 | bytes 8388608 | tf_op jit(solution)/shard_map/pallas_call | solution.py:390
  130.9 0.0 copy-start.2
  130.9 2.4 %copy.14 = bf16[128,4096]{1,0:T(8,128)(2,1)} copy(bf16[128,4096]{1,0:T(8,128)(2,1)} %get-tuple-element.8) | data formatting | bytes 2097152
  133.3 0.0 copy-done.2
  133.3 0.0 copy-start.1
  133.3 1.0 copy.15
  134.3 0.6 copy-done.1
  134.9 0.0 copy-start
  134.9 1.0 copy.16
  135.9 0.6 copy-done
  136.5 1.0 copy.17
Async XLA Ops:
  130.9 2.4 %copy-start.2 = (bf16[128,4096]{1,0:T(8,128)(2,1)S(1)}, bf16[128,4096]{1,0:T(8,128)(2,1)}, u32[]{:S(2)}) copy-start(bf16[128,4096]{1,0:T(8,128)(2,1)} %get-tuple-element.9) | copy-start | bytes 3145732
  133.3 1.6 %copy-start.1 = (bf16[128,4096]{1,0:T(8,128)(2,1)S(1)}, bf16[128,4096]{1,0:T(8,128)(2,1)}, u32[]{:S(2)}) copy-start(bf16[128,4096]{1,0:T(8,128)(2,1)} %get-tuple-element.10) | copy-start | bytes 3145732
  134.9 1.6 %copy-start = (bf16[128,4096]{1,0:T(8,128)(2,1)S(1)}, bf16[128,4096]{1,0:T(8,128)(2,1)}, u32[]{:S(2)}) copy-start(bf16[128,4096]{1,0:T(8,128)(2,1)} %get-tuple-element.11) | copy-start | bytes 3145732

commit v2 on v1

--- a/solution.py
+++ b/solution.py
@@ -35,11 +35,11 @@
 def kernel(
     G, NH, HPD, T, total_features,
     offs, gain, q_in, k_in, v_in, c_in,
-    n_out, dq_out, dk_out, dv_out,
-    stage, recv, recv_c, osta, rout, kT, vT, attT, doT, doN,
+    rout, tot,
+    xin, stage, recv, recv_c, osta, kT, vT, attT, doT, doN,
     o1, ml1, o2, ml2, dq1, dk1, dv1, dq2, dk2, dv2,
-    lse, delta, srecv, tot,
-    send_sem, recv_sem, osend_sem, orecv_sem, ssend_sem, srecv_sem,
+    lse, delta, srecv,
+    in_sem, own_sem, send_sem, recv_sem, osend_sem, orecv_sem, ssend_sem, srecv_sem,
 ):
     R = T // RES
     LEN = G * R
@@ -53,6 +53,13 @@
     base = ctx - mine
     slot = hidx * G + mine
 
+    loads = [
+        pltpu.make_async_copy(ref, xin.at[a], in_sem.at[a])
+        for a, ref in enumerate((q_in, k_in, v_in, c_in))
+    ]
+    for load in loads:
+        load.start()
+
     barrier = pltpu.get_barrier_semaphore()
 
     def greet(i, c):
@@ -69,7 +76,6 @@
     ia = lax.broadcasted_iota(jnp.int32, (T, T), 0)
     ib = lax.broadcasted_iota(jnp.int32, (T, T), 1)
     perm = jnp.where(ib == lax.rem(ia, R) * RES + ia // R, 1.0, 0.0).astype(BF16)
-    perm_t = jnp.where(ia == lax.rem(ib, R) * RES + ib // R, 1.0, 0.0).astype(BF16)
     ja = lax.broadcasted_iota(jnp.int32, (HD, HD), 0)
     jb = lax.broadcasted_iota(jnp.int32, (HD, HD), 1)
     eye_mask = ja == jb
@@ -77,9 +83,10 @@
 
     F = HPD * HD
 
-    def put_stage(a, ref):
+    def put_stage(a):
+        loads[a].wait()
         for d in range(G):
-            y = nn(perm, ref[:, d * F:(d + 1) * F]).astype(BF16)
+            y = nn(perm, xin[a, :, d * F:(d + 1) * F]).astype(BF16)
             for hh in range(HPD):
                 stage[a, d, hh] = y[:, hh * HD:(hh + 1) * HD].reshape(RES, R, HD)
 
@@ -87,7 +94,7 @@
         into = recv.at[a] if a < 3 else recv_c
 
         def one(i, c):
-            d = lax.rem(mine + i, G)
+            d = lax.rem(mine + 7 * i, G)
             pltpu.make_async_remote_copy(
                 src_ref=stage.at[a, d],
                 dst_ref=into.at[:, :, mine],
@@ -101,11 +108,11 @@
         lax.fori_loop(1, G, one, 0)
         into[:, :, mine] = stage[a, mine]
 
-    put_stage(0, q_in)
+    put_stage(0)
     pl.semaphore_wait(barrier, NP - 1)
     send_stage(0)
-    for a, ref in ((1, k_in), (2, v_in), (3, c_in)):
-        put_stage(a, ref)
+    for a in range(1, 4):
+        put_stage(a)
         send_stage(a)
 
     def offset(level, hh):
@@ -180,7 +187,9 @@
                 f2 = jnp.exp2(m2 - top)
                 total = f0 * l[:, here] + f1 * ml1[s // 2, 1, :, lanes1] + f2 * ml2[1, :, lanes2]
                 summed = f0 * o[:, here] + f1 * o1[s // 2, :, lanes1] + f2 * o2[:, lanes2]
-                attT[hh, r, :, lanes2] = (summed / total).astype(BF16)
+                att = (summed / total).astype(BF16)
+                attT[hh, r, :, lanes2] = att
+                osta[0, hh, r, pl.ds(s * SRC0, SRC0)] = turn(att).reshape(SRC0, R, HD)
                 lse[hh, r, :, lanes2] = top + jnp.log(total) * LOG2E
             return c
 
@@ -221,6 +230,23 @@
         return c
 
     lax.fori_loop(1, NP, send_stats, 0)
+
+    def send_att(i, c):
+        d = lax.rem(mine + 7 * i, G)
+        pltpu.make_async_remote_copy(
+            src_ref=osta.at[0, :, :, d],
+            dst_ref=rout.at[0, :, mine],
+            send_sem=osend_sem.at[0],
+            recv_sem=orecv_sem.at[0],
+            device_id={"ctx": base + d},
+            device_id_type=pl.DeviceIdType.MESH,
+        ).start()
+        return c
+
+    lax.fori_loop(1, G, send_att, 0)
+    own_att = pltpu.make_async_copy(osta.at[0, :, :, mine], rout.at[0, :, mine], own_sem.at[HPD])
+    own_att.start()
+
     wait_bytes(srecv.at[pl.ds(0, NP - 1)], srecv_sem)
     tot[...] = jnp.sum(srecv[...], axis=0)
 
@@ -236,7 +262,6 @@
         for hh in range(HPD):
             a = attT[hh, r].astype(F32)
             xhat = (a - mean) * inv
-            normed = (xhat * gains[hh]).astype(BF16)
             dx = doT[hh, r].astype(F32) * gains[hh]
             d = ((dx - s1 - xhat * s2) * inv).astype(BF16)
             delta[hh, r] = jnp.sum(d.astype(F32) * a, axis=0, keepdims=True)
@@ -244,23 +269,7 @@
             n = SRC0
             for s in range(SEGS0):
                 here = slice(s * W0, (s + 1) * W0)
-                osta[0, hh, r, s * n:(s + 1) * n] = turn(normed[:, here]).reshape(n, R, HD)
                 doN[hh, r, s * n:(s + 1) * n] = turn(d[:, here]).reshape(n, R, HD)
-
-    def send_normed(i, c):
-        d = lax.rem(mine + i, G)
-        pltpu.make_async_remote_copy(
-            src_ref=osta.at[0, :, :, d],
-            dst_ref=rout.at[0, :, mine],
-            send_sem=osend_sem.at[0],
-            recv_sem=orecv_sem.at[0],
-            device_id={"ctx": base + d},
-            device_id_type=pl.DeviceIdType.MESH,
-        ).start()
-        return c
-
-    lax.fori_loop(1, G, send_normed, 0)
-    rout[0, :, mine] = osta[0, :, :, mine]
 
     def backward(hh, carry):
         offsets = [offset(level, hh) for level in range(LEVELS)]
@@ -285,8 +294,7 @@
         w1 = [jnp.where(offsets[1] == r % 2, 1.0, 0.0).astype(F32) for r in range(RES)]
         w2 = [jnp.where(offsets[2] == r, 1.0, 0.0).astype(F32) for r in range(RES)]
 
-        def level0(i, c):
-            s = lax.rem(mine // SRC0 + i, SEGS0)
+        def level0(s, c):
             dq, dk, dv = segment(0, s)
             at2 = pl.ds(pl.multiple_of(s * W0, W0), W0)
             to = pl.ds(s * SRC0, SRC0)
@@ -299,41 +307,37 @@
                 osta[2, hh, r, to] = x.astype(BF16).reshape(SRC0, R, HD)
                 x = dv[here] + w1[r] * dv1[s // 2, at1] + w2[r] * dv2[at2]
                 osta[3, hh, r, to] = x.astype(BF16).reshape(SRC0, R, HD)
-            for j in range(SRC0):
-                d = s * SRC0 + j
-
-                @pl.when(d != mine)
-                def _():
-                    pltpu.make_async_remote_copy(
-                        src_ref=osta.at[pl.ds(1, 3), hh, :, d],
-                        dst_ref=rout.at[pl.ds(1, 3), hh, mine],
-                        send_sem=osend_sem.at[1 + hh],
-                        recv_sem=orecv_sem.at[1 + hh],
-                        device_id={"ctx": base + d},
-                        device_id_type=pl.DeviceIdType.MESH,
-                    ).start()
-
             return c
 
         lax.fori_loop(0, SEGS0, level0, 0)
-        rout[pl.ds(1, 3), hh, mine] = osta[pl.ds(1, 3), hh, :, mine]
+
+        def send(i, c):
+            d = lax.rem(mine + 7 * i, G)
+            pltpu.make_async_remote_copy(
+                src_ref=osta.at[pl.ds(1, 3), hh, :, d],
+                dst_ref=rout.at[pl.ds(1, 3), hh, mine],
+                send_sem=osend_sem.at[1 + hh],
+                recv_sem=orecv_sem.at[1 + hh],
+                device_id={"ctx": base + d},
+                device_id_type=pl.DeviceIdType.MESH,
+            ).start()
+            return c
+
+        lax.fori_loop(1, G, send, 0)
+        pltpu.make_async_copy(
+            osta.at[pl.ds(1, 3), hh, :, mine], rout.at[pl.ds(1, 3), hh, mine], own_sem.at[hh]
+        ).start()
         return carry
 
     lax.fori_loop(0, HPD, backward, 0)
 
-    def unpermute(ref, a, hh):
-        for g in range(G):
-            head = g * HPD + hh
-            x = nn(perm_t, rout[a, hh, g].reshape(T, HD))
-            ref[:, head * HD:(head + 1) * HD] = x.astype(BF16)
-
     wait_bytes(rout.at[0, :, pl.ds(0, G - 1)], orecv_sem.at[0])
-    for hh in range(HPD):
-        unpermute(n_out, 0, hh)
+    own_att.wait()
     for hh in range(HPD):
         wait_bytes(rout.at[pl.ds(1, 3), hh, pl.ds(0, G - 1)], orecv_sem.at[1 + hh])
-        for a, ref in ((1, dq_out), (2, dk_out), (3, dv_out)):
-            unpermute(ref, a, hh)
+        pltpu.make_async_copy(
+            osta.at[pl.ds(1, 3), hh, :, mine], rout.at[pl.ds(1, 3), hh, mine], own_sem.at[hh]
+        ).wait()
 
     for a in range(4):
         wait_bytes(stage.at[a, pl.ds(0, G - 1)], send_sem.at[a])
@@ -341,6 +345,39 @@
     wait_bytes(osta.at[0, :, :, pl.ds(0, G - 1)], osend_sem.at[0])
     for hh in range(HPD):
         wait_bytes(osta.at[pl.ds(1, 3), hh, :, pl.ds(0, G - 1)], osend_sem.at[1 + hh])
+
+
+def finish(G, HPD, T, total_features, rout, tot, gain, n_out, dq_out, dk_out, dv_out):
+    R = T // RES
+    LEN = G * R
+    mine = lax.rem(lax.axis_index("ctx"), G)
+    ia = lax.broadcasted_iota(jnp.int32, (T, T), 0)
+    ib = lax.broadcasted_iota(jnp.int32, (T, T), 1)
+    perm_t = jnp.where(ia == lax.rem(ib, R) * RES + ib // R, 1.0, 0.0).astype(BF16)
+    row = lax.broadcasted_iota(jnp.int32, (R, LEN), 0)
+    lane = lax.broadcasted_iota(jnp.int32, (R, LEN), 1)
+    own = lane == mine * R + row
+
+    def column(kind):
+        parts = [
+            jnp.sum(jnp.where(own, tot[kind * RES + r], 0.0), axis=1, keepdims=True)
+            for r in range(RES)
+        ]
+        return jnp.concatenate(parts, 0)
+
+    inv_f = 1.0 / total_features
+    mean = column(0) * inv_f
+    var = column(1) * inv_f - mean * mean
+    inv = 1.0 / jnp.sqrt(var + EPSILON)
+    for g in range(rout.shape[2]):
+        for hh in range(HPD):
+            head = g * HPD + hh
+            here = slice(head * HD, (head + 1) * HD)
+            a = rout[0, hh, g].reshape(T, HD).astype(F32)
+            normed = ((a - mean) * inv * gain[:, here]).astype(BF16)
+            n_out[:, here] = nn(perm_t, normed).astype(BF16)
+            for k, ref in ((1, dq_out), (2, dk_out), (3, dv_out)):
+                ref[:, here] = nn(perm_t, rout[k, hh, g].reshape(T, HD)).astype(BF16)
 
 
 def on_device(queries, key_rows, value_rows, offsets, sublayer_norm_gain, cotangent):
@@ -356,11 +393,11 @@
     out = jax.ShapeDtypeStruct((T, features), BF16)
     big = pltpu.VMEM((4, HPD, RES, G, R, HD), BF16)
     scratch = [
+        pltpu.VMEM((4, T, features), BF16),
         pltpu.VMEM((4, G, HPD, RES, R, HD), BF16),
         pltpu.VMEM((3, HPD, RES, G, R, HD), BF16),
         pltpu.VMEM((HPD, RES, G, R, HD), BF16),
         big,
-        pltpu.VMEM((4, HPD, G, RES, R, HD), BF16),
         pltpu.VMEM((HPD, RES, HD, LEN), BF16),
         pltpu.VMEM((RES, HD, LEN), BF16),
         pltpu.VMEM((HPD, RES, HD, LEN), BF16),
@@ -379,7 +416,8 @@
         pltpu.VMEM((HPD, RES, 1, LEN), F32),
         pltpu.VMEM((HPD, RES, 1, LEN), F32),
         pltpu.VMEM((NP, 4 * RES, 1, LEN), F32),
-        pltpu.VMEM((4 * RES, 1, LEN), F32),
+        pltpu.SemaphoreType.DMA((4,)),
+        pltpu.SemaphoreType.DMA((1 + HPD,)),
         pltpu.SemaphoreType.DMA((4,)),
         pltpu.SemaphoreType.DMA((4,)),
         pltpu.SemaphoreType.DMA((1 + HPD,)),
@@ -387,11 +425,16 @@
         pltpu.SemaphoreType.DMA,
         pltpu.SemaphoreType.DMA,
     ]
-    return pl.pallas_call(
-        functools.partial(kernel, G, NH, HPD, T, float(NH * features)),
-        out_shape=(out,) * 4,
-        in_specs=[pl.BlockSpec(memory_space=pltpu.SMEM)] + [vm] * 5,
-        out_specs=(vm,) * 4,
+    anywhere = pl.BlockSpec(memory_space=pl.ANY)
+    total_features = float(NH * features)
+    back, tot = pl.pallas_call(
+        functools.partial(kernel, G, NH, HPD, T, total_features),
+        out_shape=(
+            jax.ShapeDtypeStruct((4, HPD, G, RES, R, HD), BF16),
+            jax.ShapeDtypeStruct((4 * RES, 1, LEN), F32),
+        ),
+        in_specs=[pl.BlockSpec(memory_space=pltpu.SMEM), vm] + [anywhere] * 4,
+        out_specs=(anywhere, vm),
         scratch_shapes=scratch,
         compiler_params=pltpu.CompilerParams(
             collective_id=0, has_side_effects=True, vmem_limit_bytes=58 * 2**20
@@ -400,6 +443,23 @@
             flops=7_000_000_000, bytes_accessed=8 * 2**20, transcendentals=8_000_000
         ),
     )(offsets, sublayer_norm_gain.reshape(heads, HD), queries, key_rows, value_rows, cotangent)
+    steps = min(4, G)
+    width = features // steps
+    return pl.pallas_call(
+        functools.partial(finish, G, HPD, T, total_features),
+        grid=(steps,),
+        out_shape=(out,) * 4,
+        in_specs=[
+            pl.BlockSpec((4, HPD, G // steps, RES, R, HD), lambda i: (0, 0, i, 0, 0, 0)),
+            pl.BlockSpec((4 * RES, 1, LEN), lambda i: (0, 0, 0)),
+            pl.BlockSpec((1, width), lambda i: (0, i)),
+        ],
+        out_specs=(pl.BlockSpec((T, width), lambda i: (0, i)),) * 4,
+        compiler_params=pltpu.CompilerParams(vmem_limit_bytes=58 * 2**20),
+        cost_estimate=pl.CostEstimate(
+            flops=8 * T * T * features, bytes_accessed=8 * 2**20, transcendentals=0
+        ),
+    )(back, tot, sublayer_norm_gain.reshape(1, features))
 
 
 def solution(mesh):

time: 138 us -> 116 us (0.84)
  the two profiles are of different devices: /device:TPU:7 before, /device:TPU:1 now
where the time goes in v2:
time: 116 us
  Pallas kernels  115 us (99%)
    pallas_call x1, Pallas kernels, on_device(): pl.pallas_call(functools.partial(kernel, G, NH, HPD, T, total_features),...  109 us
    pallas_call x1, Pallas kernels, on_device(): pl.pallas_call(functools.partial(finish, G, HPD, T, total_features), grid...  5.76 us

profile of v2, /device:TPU:1, one launch (start us, length us, event | category | flops | bytes accessed | tf_op | source)
XLA Modules:
  0.0 115.8 jit_solution(18302794865350960899)
XLA Ops:
  0.6 109.4 %shard_map.93 = (bf16[4,2,16,4,32,128]{5,4,3,2,1,0:T(8,128)(2,1)}, f32[16,1,512]{2,1,0:T(1,128)}) custom-call(s32[3,32]{1,0:T(4,128)} %offs.1, f32[32,128]{1,0:T(8,128)} %bitcast.2, bf16[128,4096]{1,0:T(8,128)(2,1)} %q_in.1, bf16[128,4096]{1,0:T(8,128)(2,1)} %k_in.1, bf16[128,4096]{1,0:T(8,128)(2,1)} %v_in.1, bf16[128,4096]{1,0:T(8,128)(2,1)} %c_in.1), custom_call_target="tpu_custom_call" | custom-call | flops 7000000000 | bytes 8388608 | tf_op jit(solution)/shard_map/pallas_call | solution.py:430
  110.0 5.8 %shard_map.94 = (bf16[128,4096]{1,0:T(8,128)(2,1)}, bf16[128,4096]{1,0:T(8,128)(2,1)}, bf16[128,4096]{1,0:T(8,128)(2,1)}, bf16[128,4096]{1,0:T(8,128)(2,1)}) custom-call(bf16[4,2,16,4,32,128]{5,4,3,2,1,0:T(8,128)(2,1)} %get-tuple-element.6.rout, f32[16,1,512]{2,1,0:T(1,128)} %get-tuple-element.7.tot, f32[1,4096]{1,0:T(1,128)} %bitcast.3), custom_call_target="tpu_custom_call" | custom-call | flops 536870912 | bytes 8388608 | tf_op jit(solution)/shard_map/pallas_call | solution.py:448

commit v3 on v2

--- a/solution.py
+++ b/solution.py
@@ -38,13 +38,14 @@
     rout, tot,
     xin, stage, recv, recv_c, osta, kT, vT, attT, doT, doN,
     o1, ml1, o2, ml2, dq1, dk1, dv1, dq2, dk2, dv2,
-    lse, delta, srecv,
-    in_sem, own_sem, send_sem, recv_sem, osend_sem, orecv_sem, ssend_sem, srecv_sem,
+    lse, delta, part_sums, srecv, sums_all,
+    in_sem, own_sem, send_sem, recv_sem, osend_sem, orecv_sem, ssend_sem, srecv_sem, gsend_sem, grecv_sem,
 ):
     R = T // RES
     LEN = G * R
     NP = G * NH
     SRC0 = SEG0 // T
+    ROWS = 4 * RES // G
     W0 = SRC0 * R
     SEGS0 = G // SRC0
     ctx = lax.axis_index("ctx")
@@ -215,12 +216,12 @@
             part = [jnp.sum(x, axis=0, keepdims=True) for x in (a, a * a, dx, dx * a)]
             sums = part if sums is None else [x + y for x, y in zip(sums, part)]
         for kind in range(4):
-            srecv[slot, kind * RES + r] = sums[kind]
+            part_sums[kind * RES + r] = sums[kind]
 
     def send_stats(i, c):
         peer = lax.rem(slot + i, NP)
         pltpu.make_async_remote_copy(
-            src_ref=srecv.at[slot],
+            src_ref=part_sums.at[pl.ds(lax.rem(peer, G) * ROWS, ROWS)],
             dst_ref=srecv.at[slot],
             send_sem=ssend_sem,
             recv_sem=srecv_sem,
@@ -230,6 +231,23 @@
         return c
 
     lax.fori_loop(1, NP, send_stats, 0)
+    srecv[slot] = part_sums[pl.ds(mine * ROWS, ROWS)]
+    wait_bytes(srecv.at[pl.ds(0, NP - 1)], srecv_sem)
+    own_rows = pl.ds(mine * ROWS, ROWS)
+    sums_all[own_rows] = jnp.sum(srecv[...], axis=0)
+
+    def send_sums(i, c):
+        pltpu.make_async_remote_copy(
+            src_ref=sums_all.at[own_rows],
+            dst_ref=sums_all.at[own_rows],
+            send_sem=gsend_sem,
+            recv_sem=grecv_sem,
+            device_id={"ctx": base + lax.rem(mine + i, G)},
+            device_id_type=pl.DeviceIdType.MESH,
+        ).start()
+        return c
+
+    lax.fori_loop(1, G, send_sums, 0)
 
     def send_att(i, c):
         d = lax.rem(mine + 7 * i, G)
@@ -247,8 +265,8 @@
     own_att = pltpu.make_async_copy(osta.at[0, :, :, mine], rout.at[0, :, mine], own_sem.at[HPD])
     own_att.start()
 
-    wait_bytes(srecv.at[pl.ds(0, NP - 1)], srecv_sem)
-    tot[...] = jnp.sum(srecv[...], axis=0)
+    wait_bytes(sums_all.at[pl.ds(0, (G - 1) * ROWS)], grecv_sem)
+    tot[...] = sums_all[...]
 
     inv_f = 1.0 / total_features
     for r in range(RES):
@@ -342,6 +360,7 @@
     for a in range(4):
         wait_bytes(stage.at[a, pl.ds(0, G - 1)], send_sem.at[a])
     wait_bytes(srecv.at[pl.ds(0, NP - 1)], ssend_sem)
+    wait_bytes(sums_all.at[pl.ds(0, (G - 1) * ROWS)], gsend_sem)
     wait_bytes(osta.at[0, :, :, pl.ds(0, G - 1)], osend_sem.at[0])
     for hh in range(HPD):
         wait_bytes(osta.at[pl.ds(1, 3), hh, :, pl.ds(0, G - 1)], osend_sem.at[1 + hh])
@@ -369,15 +388,15 @@
     mean = column(0) * inv_f
     var = column(1) * inv_f - mean * mean
     inv = 1.0 / jnp.sqrt(var + EPSILON)
-    for g in range(rout.shape[2]):
-        for hh in range(HPD):
-            head = g * HPD + hh
-            here = slice(head * HD, (head + 1) * HD)
-            a = rout[0, hh, g].reshape(T, HD).astype(F32)
-            normed = ((a - mean) * inv * gain[:, here]).astype(BF16)
-            n_out[:, here] = nn(perm_t, normed).astype(BF16)
-            for k, ref in ((1, dq_out), (2, dk_out), (3, dv_out)):
-                ref[:, here] = nn(perm_t, rout[k, hh, g].reshape(T, HD)).astype(BF16)
+    for g in range(0, rout.shape[2], 2):
+        heads = [(g + j, hh) for j in range(2) for hh in range(HPD)]
+        here = slice(g * HPD * HD, (g + 2) * HPD * HD)
+        a = jnp.concatenate([rout[0, hh, j].reshape(T, HD) for j, hh in heads], 1).astype(F32)
+        normed = ((a - mean) * inv * gain[:, here]).astype(BF16)
+        n_out[:, here] = nn(perm_t, normed).astype(BF16)
+        for k, ref in ((1, dq_out), (2, dk_out), (3, dv_out)):
+            x = jnp.concatenate([rout[k, hh, j].reshape(T, HD) for j, hh in heads], 1)
+            ref[:, here] = nn(perm_t, x).astype(BF16)
 
 
 def on_device(queries, key_rows, value_rows, offsets, sublayer_norm_gain, cotangent):
@@ -415,13 +434,17 @@
         pltpu.VMEM((SEG0, HD), F32),
         pltpu.VMEM((HPD, RES, 1, LEN), F32),
         pltpu.VMEM((HPD, RES, 1, LEN), F32),
-        pltpu.VMEM((NP, 4 * RES, 1, LEN), F32),
+        pltpu.VMEM((4 * RES, 1, LEN), F32),
+        pltpu.VMEM((NP, 4 * RES // G, 1, LEN), F32),
+        pltpu.VMEM((4 * RES, 1, LEN), F32),
         pltpu.SemaphoreType.DMA((4,)),
         pltpu.SemaphoreType.DMA((1 + HPD,)),
         pltpu.SemaphoreType.DMA((4,)),
         pltpu.SemaphoreType.DMA((4,)),
         pltpu.SemaphoreType.DMA((1 + HPD,)),
         pltpu.SemaphoreType.DMA((1 + HPD,)),
+        pltpu.SemaphoreType.DMA,
+        pltpu.SemaphoreType.DMA,
         pltpu.SemaphoreType.DMA,
         pltpu.SemaphoreType.DMA,
     ]

time: 116 us -> 114 us (0.983)
  Pallas kernels: 115 us -> 113 us
    pallas_call x1, Pallas kernels: 109 us -> 107 us  [on_device(): pl.pallas_call(functools.partial(kernel, G, NH, HPD, T, total_features),...]
where the time goes in v3:
time: 114 us; the launch traced here: 113 us
  Pallas kernels  113 us (99%)
    pallas_call x1, Pallas kernels, on_device(): pl.pallas_call(functools.partial(kernel, G, NH, HPD, T, total_features),...  107 us
    pallas_call x1, Pallas kernels, on_device(): pl.pallas_call(functools.partial(finish, G, HPD, T, total_features), grid...  5.72 us

profile of v3, /device:TPU:1, one launch (start us, length us, event | category | flops | bytes accessed | tf_op | source)
XLA Modules:
  0.0 113.4 jit_solution(13993844981734951017)
XLA Ops:
  0.6 107.0 %shard_map.93 = (bf16[4,2,16,4,32,128]{5,4,3,2,1,0:T(8,128)(2,1)}, f32[16,1,512]{2,1,0:T(1,128)}) custom-call(s32[3,32]{1,0:T(4,128)} %offs.1, f32[32,128]{1,0:T(8,128)} %bitcast.2, bf16[128,4096]{1,0:T(8,128)(2,1)} %q_in.1, bf16[128,4096]{1,0:T(8,128)(2,1)} %k_in.1, bf16[128,4096]{1,0:T(8,128)(2,1)} %v_in.1, bf16[128,4096]{1,0:T(8,128)(2,1)} %c_in.1), custom_call_target="tpu_custom_call" | custom-call | flops 7000000000 | bytes 8388608 | tf_op jit(solution)/shard_map/pallas_call | solution.py:453
  107.7 5.7 %shard_map.94 = (bf16[128,4096]{1,0:T(8,128)(2,1)}, bf16[128,4096]{1,0:T(8,128)(2,1)}, bf16[128,4096]{1,0:T(8,128)(2,1)}, bf16[128,4096]{1,0:T(8,128)(2,1)}) custom-call(bf16[4,2,16,4,32,128]{5,4,3,2,1,0:T(8,128)(2,1)} %get-tuple-element.6.rout, f32[16,1,512]{2,1,0:T(1,128)} %get-tuple-element.7.tot, f32[1,4096]{1,0:T(1,128)} %bitcast.3), custom_call_target="tpu_custom_call" | custom-call | flops 536870912 | bytes 8388608 | tf_op jit(solution)/shard_map/pallas_call | solution.py:471
